TPU v7x, 128 devices: a whole 4x4x4 slice. The times are simulated.
128 devices in a mesh: wide: 16 (over z, x), narrow: 8 (over y, core).
Axes of the slice: x: 4, y: 4, z: 4, core: 2. Of those that a mesh axis runs over, the one named last changes fastest.
Arguments:
- scalars: float32 [16384, 16, 128], P(('wide', 'narrow')), may hold values from -6 to 6
- mass: float32 [16384, 128], P(('wide', 'narrow')), may hold values from 0.2 to 5
- frequency: float32 [16384, 128], P(('wide', 'narrow')), may hold values from 0.02 to 4
- cell: int32 [16384, 128], P(('wide', 'narrow')), may hold values from 0 to 1299
- owner: int32 [16384, 1], P(('wide', 'narrow')), may hold values from 0 to 127; in each aligned block of 128 rows (0 to 127, 128 to 255, ...) at most 2 rows name the same one
Outputs:
- mixed: float32 [16384, 16, 128], P(('wide', 'narrow'))
- cell_mean: float32 [16, 128, 1024], P(None, 'wide', 'narrow')
Inputs may be any that keep to these rules, and one draw needn't show every extreme that they name: The blocks of one device name any one owner at most 2 times, a bound that some block reaches.
All inputs are finite; a program needn't handle non-finite values.
Results may differ from a plain program's by a relative error of at most 0.000084.
Values sent between devices are 32-bit elements; how exact they have to be, the bound alone decides.
A program may use at most 64 MiB of HBM per device.

v0:
```python
import math

import jax
import jax.numpy as jnp
from jax import lax
from jax.sharding import PartitionSpec as P

CW = 8
CN = 128


def shifted(shard, axis, by):
    length = lax.axis_size(axis)
    return lax.ppermute(shard, axis, [(i, (i + by) % length) for i in range(length)])


def with_halo(cells, sides, width):
    for axis, dim in sides:
        count = lax.axis_size(axis)
        head = lax.slice_in_dim(cells, 0, width, axis=dim)
        tail = lax.slice_in_dim(cells, cells.shape[dim] - width, cells.shape[dim], axis=dim)
        cells = jnp.concatenate(
            [
                lax.ppermute(tail, axis, [(i, (i + 1) % count) for i in range(count)]),
                cells,
                lax.ppermute(head, axis, [((i + 1) % count, i) for i in range(count)]),
            ],
            axis=dim,
        )
    return cells


def table_for(cells, extent):
    return (cells[:, None] == jnp.arange(extent, dtype=jnp.int32)[None, :]).astype(jnp.float32)


def per_device(scalars, mass, frequency, cell, owner):
    wide_count = lax.axis_size("wide")
    narrow_count = lax.axis_size("narrow")
    devices_all = wide_count * narrow_count
    block_count = scalars.shape[0]
    scalar_count = scalars.shape[1]
    per_block = scalars.shape[2]
    extent = (CW + 2) * (CN + 2)
    capacity = max(2, (2 * block_count + devices_all - 1) // devices_all)
    slot_total = devices_all * capacity
    group = math.gcd(slot_total, 16)
    group_rows = group * per_block
    group_count = slot_total // group
    target = owner[:, 0]
    matches = (target[:, None] == jnp.arange(devices_all, dtype=jnp.int32)[None, :]).astype(
        jnp.int32
    )
    position = jnp.sum((jnp.cumsum(matches, axis=0) - matches) * matches, axis=1)
    slot_index = target * capacity + position
    payload = jnp.concatenate(
        [scalars, mass[:, None, :], frequency[:, None, :], cell.astype(jnp.float32)[:, None, :]],
        axis=1,
    )
    outgoing = (
        jnp.zeros((slot_total, scalar_count + 3, per_block), jnp.float32)
        .at[slot_index]
        .set(payload)
    )
    arrived = lax.all_to_all(outgoing, ("wide", "narrow"), split_axis=0, concat_axis=0, tiled=True)
    phi_here = arrived[:, :scalar_count, :]
    mass_here = arrived[:, scalar_count, :]
    rate_here = arrived[:, scalar_count + 1, :]
    cell_here = arrived[:, scalar_count + 2, :].astype(jnp.int32)
    moving = jnp.concatenate([phi_here * mass_here[:, None, :], mass_here[:, None, :]], axis=1)

    def deposit_group(index, total):
        start = index * group
        piece = lax.dynamic_slice_in_dim(moving, start, group, 0)
        cells = lax.dynamic_slice_in_dim(cell_here, start, group, 0).reshape(group_rows)
        onehot = table_for(cells, extent)
        rows = jnp.transpose(piece, (1, 0, 2)).reshape(scalar_count + 1, group_rows)
        return total + jnp.dot(
            rows, onehot, preferred_element_type=jnp.float32, precision=lax.Precision.HIGHEST
        )

    deposit = lax.fori_loop(
        0, group_count, deposit_group, jnp.zeros((scalar_count + 1, extent), jnp.float32)
    )
    partial_value = deposit.reshape(scalar_count + 1, CW + 2, CN + 2)
    from_before = shifted(partial_value[:, CW + 1 : CW + 2, :], "wide", 1)
    from_after = shifted(partial_value[:, 0:1, :], "wide", -1)
    summed = partial_value[:, 1 : CW + 1, :]
    summed = summed.at[:, 0:1, :].add(from_before).at[:, CW - 1 : CW, :].add(from_after)
    side_before = shifted(summed[:, :, CN + 1 : CN + 2], "narrow", 1)
    side_after = shifted(summed[:, :, 0:1], "narrow", -1)
    inner = summed[:, :, 1 : CN + 1]
    inner = inner.at[:, :, 0:1].add(side_before).at[:, :, CN - 1 : CN].add(side_after)
    mean_inner = inner[:scalar_count] / (inner[scalar_count] + 1.0)
    mean_cycle = with_halo(mean_inner, (("wide", 1), ("narrow", 2)), 1)
    mean_flat = mean_cycle.reshape(scalar_count, extent)

    def read_group(index, gathered):
        start = index * group
        cells = lax.dynamic_slice_in_dim(cell_here, start, group, 0).reshape(group_rows)
        onehot = table_for(cells, extent)
        values = lax.dot_general(
            mean_flat,
            onehot,
            (((1,), (1,)), ((), ())),
            preferred_element_type=jnp.float32,
            precision=lax.Precision.HIGHEST,
        )
        values = jnp.transpose(values.reshape(scalar_count, group, per_block), (1, 0, 2))
        return lax.dynamic_update_slice_in_dim(gathered, values, start, 0)

    near = lax.fori_loop(
        0, group_count, read_group, jnp.zeros((slot_total, scalar_count, per_block), jnp.float32)
    )
    decay = jnp.exp(-rate_here * (1.5 + jnp.tanh(near[:, 0, :])))
    mixed_here = near + (phi_here - near) * decay[:, None, :]
    returned = lax.all_to_all(
        mixed_here, ("wide", "narrow"), split_axis=0, concat_axis=0, tiled=True
    )
    mixed = jnp.take(returned, slot_index, axis=0)
    return (mixed, mean_inner)


def solution(mesh):
    return jax.shard_map(
        per_device,
        mesh=mesh,
        in_specs=(
            P(("wide", "narrow"), None, None),
            P(("wide", "narrow"), None),
            P(("wide", "narrow"), None),
            P(("wide", "narrow"), None),
            P(("wide", "narrow"), None),
        ),
        out_specs=(P(("wide", "narrow"), None, None), P(None, "wide", "narrow")),
        check_vma=False,
    )
```

profile of v0, /device:TPU:1, one launch (start us, length us, event | category | flops | bytes accessed | tf_op | source)
XLA Modules:
  0.0 369.1 jit_solution(14848168411799421609)
XLA Ops:
  7.3 15.6 %scatter_fusion = f32[256,19,128]{2,1,0:T(8,128)} fusion(f32[256,19,128]{2,1,0:T(8,128)} %broadcast_in_dim.40, s32[128]{0:T(128)S(1)} %bitcast.73, f32[128,19,128]{2,1,0:T(8,128)S(1)} %pad_maximum_fusion.1), kind=kCustom, calls=%fused_computation.1 | custom fusion | bytes 3736064 | tf_op jit(solution)/shard_map/scatter | solution.py:63
  22.8 11.5 %all-to-all-start = ((f32[256,19,128]{2,1,0:T(8,128)}), f32[256,19,128]{2,1,0:T(8,128)S(1)}, u32[]{:S(2)}, u32[]{:S(2)}) async-start(f32[256,19,128]{2,1,0:T(8,128)} %scatter_fusion), calls=%async_computation | async-start | bytes 6291456 | tf_op jit(solution)/shard_map/all_to_all | solution.py:65
  34.4 41.9 %all-to-all-done = f32[256,19,128]{2,1,0:T(8,128)S(1)} async-done(((f32[256,19,128]{2,1,0:T(8,128)}), f32[256,19,128]{2,1,0:T(8,128)S(1)}, u32[]{:S(2)}, u32[]{:S(2)}) %all-to-all-start) | async-done | bytes 2490400 | tf_op jit(solution)/shard_map/all_to_all | solution.py:65
  79.5 99.8 %while.32 = (s32[]{:T(128)}, f32[17,1300]{1,0:T(8,128)}, f32[256,17,128]{2,0,1:T(8,128)}, s32[256,128]{1,0:T(8,128)S(1)}, s32[]{:T(128)}, /*index=5*/s32[]{:T(128)}, s32[]{:T(128)}, s32[]{:T(128)}, f32[]{:T(128)}) while((s32[]{:T(128)}, f32[17,1300]{1,0:T(8,128)}, f32[256,17,128]{2,0,1:T(8,128)}, s32[256,128]{1,0:T(8,128)S(1)}, ...), condition=%wide.region_4.5_spmd.clone, body=%wide.region_3.4_spmd.clone.sunk | while | flops 545836160 | bytes 1348417 | solution.py:82
  98.5 5.3 %fusion.22 = f32[17,1300]{1,0:T(8,128)} fusion(f32[17,2048]{1,0:T(8,128)S(1)} %bitcast.64, s32[2048]{0:T(1024)S(1)} %dynamic-slice_bitcast_fusion.8, f32[17,1300]{1,0:T(8,128)} %get-tuple-element.326, pred[]{:T(512)S(6)} %compare.25), kind=kOutput, calls=%fused_computation.11.clone.1 | convolution fusion | flops 545836160 | bytes 324257 | tf_op jit(solution)/shard_map/while/body/eval_jaxpr/dot_general | solution.py:78
  104.8 5.3 %fusion.22 = f32[17,1300]{1,0:T(8,128)} fusion(f32[17,2048]{1,0:T(8,128)S(1)} %bitcast.64, s32[2048]{0:T(1024)S(1)} %dynamic-slice_bitcast_fusion.8, f32[17,1300]{1,0:T(8,128)} %get-tuple-element.326, pred[]{:T(512)S(6)} %compare.25), kind=kOutput, calls=%fused_computation.11.clone.1 | convolution fusion | flops 545836160 | bytes 324257 | tf_op jit(solution)/shard_map/while/body/eval_jaxpr/dot_general | solution.py:78
  111.1 5.3 %fusion.22 = f32[17,1300]{1,0:T(8,128)} fusion(f32[17,2048]{1,0:T(8,128)S(1)} %bitcast.64, s32[2048]{0:T(1024)S(1)} %dynamic-slice_bitcast_fusion.8, f32[17,1300]{1,0:T(8,128)} %get-tuple-element.326, pred[]{:T(512)S(6)} %compare.25), kind=kOutput, calls=%fused_computation.11.clone.1 | convolution fusion | flops 545836160 | bytes 324257 | tf_op jit(solution)/shard_map/while/body/eval_jaxpr/dot_general | solution.py:78
  136.2 5.3 %fusion.22 = f32[17,1300]{1,0:T(8,128)} fusion(f32[17,2048]{1,0:T(8,128)S(1)} %bitcast.64, s32[2048]{0:T(1024)S(1)} %dynamic-slice_bitcast_fusion.8, f32[17,1300]{1,0:T(8,128)} %get-tuple-element.326, pred[]{:T(512)S(6)} %compare.25), kind=kOutput, calls=%fused_computation.11.clone.1 | convolution fusion | flops 545836160 | bytes 324257 | tf_op jit(solution)/shard_map/while/body/eval_jaxpr/dot_general | solution.py:78
  142.5 5.3 %fusion.22 = f32[17,1300]{1,0:T(8,128)} fusion(f32[17,2048]{1,0:T(8,128)S(1)} %bitcast.64, s32[2048]{0:T(1024)S(1)} %dynamic-slice_bitcast_fusion.8, f32[17,1300]{1,0:T(8,128)} %get-tuple-element.326, pred[]{:T(512)S(6)} %compare.25), kind=kOutput, calls=%fused_computation.11.clone.1 | convolution fusion | flops 545836160 | bytes 324257 | tf_op jit(solution)/shard_map/while/body/eval_jaxpr/dot_general | solution.py:78
  148.8 5.3 %fusion.22 = f32[17,1300]{1,0:T(8,128)} fusion(f32[17,2048]{1,0:T(8,128)S(1)} %bitcast.64, s32[2048]{0:T(1024)S(1)} %dynamic-slice_bitcast_fusion.8, f32[17,1300]{1,0:T(8,128)} %get-tuple-element.326, pred[]{:T(512)S(6)} %compare.25), kind=kOutput, calls=%fused_computation.11.clone.1 | convolution fusion | flops 545836160 | bytes 324257 | tf_op jit(solution)/shard_map/while/body/eval_jaxpr/dot_general | solution.py:78
  155.1 5.3 %fusion.22 = f32[17,1300]{1,0:T(8,128)} fusion(f32[17,2048]{1,0:T(8,128)S(1)} %bitcast.64, s32[2048]{0:T(1024)S(1)} %dynamic-slice_bitcast_fusion.8, f32[17,1300]{1,0:T(8,128)} %get-tuple-element.326, pred[]{:T(512)S(6)} %compare.25), kind=kOutput, calls=%fused_computation.11.clone.1 | convolution fusion | flops 545836160 | bytes 324257 | tf_op jit(solution)/shard_map/while/body/eval_jaxpr/dot_general | solution.py:78
  174.0 5.3 %fusion.22 = f32[17,1300]{1,0:T(8,128)} fusion(f32[17,2048]{1,0:T(8,128)S(1)} %bitcast.64, s32[2048]{0:T(1024)S(1)} %dynamic-slice_bitcast_fusion.8, f32[17,1300]{1,0:T(8,128)} %get-tuple-element.326, pred[]{:T(512)S(6)} %compare.25), kind=kOutput, calls=%fused_computation.11.clone.1 | convolution fusion | flops 545836160 | bytes 324257 | tf_op jit(solution)/shard_map/while/body/eval_jaxpr/dot_general | solution.py:78
  197.3 5.3 %collective-permute-start.5 = (f32[16,1,128]{2,1,0:T(1,128)S(1)}, f32[16,1,128]{2,1,0:T(1,128)S(1)}, u32[]{:S(2)}, u32[]{:S(2)}) collective-permute-start(f32[16,1,128]{2,1,0:T(1,128)S(1)} %get-tuple-element.265), channel_id=1, source_target_pairs={{8,0},{16,8},{24,16},{32,24},{40,32},{48,40},{56,48},{64,56},{72,6... | collective-permute-start | bytes 24584 | tf_op jit(solution)/shard_map/ppermute | solution.py:26
  213.0 107.1 %while.31 = (s32[]{:T(128)}, f32[256,16,128]{2,0,1:T(8,128)}, s32[256,128]{1,0:T(8,128)}, f32[16,1300]{1,0:T(8,128)S(1)}, s32[]{:T(128)}, /*index=5*/s32[]{:T(128)}, s32[]{:T(128)}, s32[]{:T(128)}) while((s32[]{:T(128)}, f32[256,16,128]{2,0,1:T(8,128)}, s32[256,128]{1,0:T(8,128)}, f32[16,1300]{1,0:T(8,128)S(1)}, s32[]{:T(128)}, ...), condition=%wide.region_6.7_spmd, body=%wide.region_5.6_spmd.sunk | while | flops 513843200 | bytes 763275 | solution.py:112
  213.7 5.3 %fusion.20 = f32[2,8,16,128]{3,1,2,0:T(8,128)S(1)} fusion(f32[16,1300]{1,0:T(8,128)S(1)} %get-tuple-element.362, s32[2048]{0:T(1024)S(1)} %dynamic-slice_bitcast_fusion.6), kind=kOutput, calls=%fused_computation.5.clone.1 | convolution fusion | flops 513843200 | bytes 222464 | tf_op jit(solution)/shard_map/while/body/eval_jaxpr/dot_general | solution.py:102
  220.4 5.3 %fusion.20 = f32[2,8,16,128]{3,1,2,0:T(8,128)S(1)} fusion(f32[16,1300]{1,0:T(8,128)S(1)} %get-tuple-element.362, s32[2048]{0:T(1024)S(1)} %dynamic-slice_bitcast_fusion.6), kind=kOutput, calls=%fused_computation.5.clone.1 | convolution fusion | flops 513843200 | bytes 222464 | tf_op jit(solution)/shard_map/while/body/eval_jaxpr/dot_general | solution.py:102
  227.1 5.3 %fusion.20 = f32[2,8,16,128]{3,1,2,0:T(8,128)S(1)} fusion(f32[16,1300]{1,0:T(8,128)S(1)} %get-tuple-element.362, s32[2048]{0:T(1024)S(1)} %dynamic-slice_bitcast_fusion.6), kind=kOutput, calls=%fused_computation.5.clone.1 | convolution fusion | flops 513843200 | bytes 222464 | tf_op jit(solution)/shard_map/while/body/eval_jaxpr/dot_general | solution.py:102
  233.8 5.3 %fusion.20 = f32[2,8,16,128]{3,1,2,0:T(8,128)S(1)} fusion(f32[16,1300]{1,0:T(8,128)S(1)} %get-tuple-element.362, s32[2048]{0:T(1024)S(1)} %dynamic-slice_bitcast_fusion.6), kind=kOutput, calls=%fused_computation.5.clone.1 | convolution fusion | flops 513843200 | bytes 222464 | tf_op jit(solution)/shard_map/while/body/eval_jaxpr/dot_general | solution.py:102
  240.5 5.3 %fusion.20 = f32[2,8,16,128]{3,1,2,0:T(8,128)S(1)} fusion(f32[16,1300]{1,0:T(8,128)S(1)} %get-tuple-element.362, s32[2048]{0:T(1024)S(1)} %dynamic-slice_bitcast_fusion.6), kind=kOutput, calls=%fused_computation.5.clone.1 | convolution fusion | flops 513843200 | bytes 222464 | tf_op jit(solution)/shard_map/while/body/eval_jaxpr/dot_general | solution.py:102
  247.2 5.3 %fusion.20 = f32[2,8,16,128]{3,1,2,0:T(8,128)S(1)} fusion(f32[16,1300]{1,0:T(8,128)S(1)} %get-tuple-element.362, s32[2048]{0:T(1024)S(1)} %dynamic-slice_bitcast_fusion.6), kind=kOutput, calls=%fused_computation.5.clone.1 | convolution fusion | flops 513843200 | bytes 222464 | tf_op jit(solution)/shard_map/while/body/eval_jaxpr/dot_general | solution.py:102
  253.9 5.3 %fusion.20 = f32[2,8,16,128]{3,1,2,0:T(8,128)S(1)} fusion(f32[16,1300]{1,0:T(8,128)S(1)} %get-tuple-element.362, s32[2048]{0:T(1024)S(1)} %dynamic-slice_bitcast_fusion.6), kind=kOutput, calls=%fused_computation.5.clone.1 | convolution fusion | flops 513843200 | bytes 222464 | tf_op jit(solution)/shard_map/while/body/eval_jaxpr/dot_general | solution.py:102
  260.6 5.3 %fusion.20 = f32[2,8,16,128]{3,1,2,0:T(8,128)S(1)} fusion(f32[16,1300]{1,0:T(8,128)S(1)} %get-tuple-element.362, s32[2048]{0:T(1024)S(1)} %dynamic-slice_bitcast_fusion.6), kind=kOutput, calls=%fused_computation.5.clone.1 | convolution fusion | flops 513843200 | bytes 222464 | tf_op jit(solution)/shard_map/while/body/eval_jaxpr/dot_general | solution.py:102
  267.2 5.3 %fusion.20 = f32[2,8,16,128]{3,1,2,0:T(8,128)S(1)} fusion(f32[16,1300]{1,0:T(8,128)S(1)} %get-tuple-element.362, s32[2048]{0:T(1024)S(1)} %dynamic-slice_bitcast_fusion.6), kind=kOutput, calls=%fused_computation.5.clone.1 | convolution fusion | flops 513843200 | bytes 222464 | tf_op jit(solution)/shard_map/while/body/eval_jaxpr/dot_general | solution.py:102
  273.9 5.3 %fusion.20 = f32[2,8,16,128]{3,1,2,0:T(8,128)S(1)} fusion(f32[16,1300]{1,0:T(8,128)S(1)} %get-tuple-element.362, s32[2048]{0:T(1024)S(1)} %dynamic-slice_bitcast_fusion.6), kind=kOutput, calls=%fused_computation.5.clone.1 | convolution fusion | flops 513843200 | bytes 222464 | tf_op jit(solution)/shard_map/while/body/eval_jaxpr/dot_general | solution.py:102
  280.6 5.3 %fusion.20 = f32[2,8,16,128]{3,1,2,0:T(8,128)S(1)} fusion(f32[16,1300]{1,0:T(8,128)S(1)} %get-tuple-element.362, s32[2048]{0:T(1024)S(1)} %dynamic-slice_bitcast_fusion.6), kind=kOutput, calls=%fused_computation.5.clone.1 | convolution fusion | flops 513843200 | bytes 222464 | tf_op jit(solution)/shard_map/while/body/eval_jaxpr/dot_general | solution.py:102
  287.3 5.3 %fusion.20 = f32[2,8,16,128]{3,1,2,0:T(8,128)S(1)} fusion(f32[16,1300]{1,0:T(8,128)S(1)} %get-tuple-element.362, s32[2048]{0:T(1024)S(1)} %dynamic-slice_bitcast_fusion.6), kind=kOutput, calls=%fused_computation.5.clone.1 | convolution fusion | flops 513843200 | bytes 222464 | tf_op jit(solution)/shard_map/while/body/eval_jaxpr/dot_general | solution.py:102
  294.0 5.3 %fusion.20 = f32[2,8,16,128]{3,1,2,0:T(8,128)S(1)} fusion(f32[16,1300]{1,0:T(8,128)S(1)} %get-tuple-element.362, s32[2048]{0:T(1024)S(1)} %dynamic-slice_bitcast_fusion.6), kind=kOutput, calls=%fused_computation.5.clone.1 | convolution fusion | flops 513843200 | bytes 222464 | tf_op jit(solution)/shard_map/while/body/eval_jaxpr/dot_general | solution.py:102
  300.7 5.3 %fusion.20 = f32[2,8,16,128]{3,1,2,0:T(8,128)S(1)} fusion(f32[16,1300]{1,0:T(8,128)S(1)} %get-tuple-element.362, s32[2048]{0:T(1024)S(1)} %dynamic-slice_bitcast_fusion.6), kind=kOutput, calls=%fused_computation.5.clone.1 | convolution fusion | flops 513843200 | bytes 222464 | tf_op jit(solution)/shard_map/while/body/eval_jaxpr/dot_general | solution.py:102
  307.4 5.3 %fusion.20 = f32[2,8,16,128]{3,1,2,0:T(8,128)S(1)} fusion(f32[16,1300]{1,0:T(8,128)S(1)} %get-tuple-element.362, s32[2048]{0:T(1024)S(1)} %dynamic-slice_bitcast_fusion.6), kind=kOutput, calls=%fused_computation.5.clone.1 | convolution fusion | flops 513843200 | bytes 222464 | tf_op jit(solution)/shard_map/while/body/eval_jaxpr/dot_general | solution.py:102
  314.1 5.3 %fusion.20 = f32[2,8,16,128]{3,1,2,0:T(8,128)S(1)} fusion(f32[16,1300]{1,0:T(8,128)S(1)} %get-tuple-element.362, s32[2048]{0:T(1024)S(1)} %dynamic-slice_bitcast_fusion.6), kind=kOutput, calls=%fused_computation.5.clone.1 | convolution fusion | flops 513843200 | bytes 222464 | tf_op jit(solution)/shard_map/while/body/eval_jaxpr/dot_general | solution.py:102
  325.3 11.4 %all-to-all-start.1 = ((f32[256,16,128]{2,1,0:T(8,128)}), f32[256,16,128]{2,1,0:T(8,128)S(1)}, u32[]{:S(2)}, u32[]{:S(2)}) async-start(f32[256,16,128]{2,1,0:T(8,128)} %multiply_add_fusion), calls=%async_computation.1 | async-start | bytes 4194304 | tf_op jit(solution)/shard_map/all_to_all | solution.py:117
  336.6 30.5 %all-to-all-done.1 = f32[256,16,128]{2,1,0:T(8,128)S(1)} async-done(((f32[256,16,128]{2,1,0:T(8,128)}), f32[256,16,128]{2,1,0:T(8,128)S(1)}, u32[]{:S(2)}, u32[]{:S(2)}) %all-to-all-start.1) | async-done | bytes 2097184 | tf_op jit(solution)/shard_map/all_to_all | solution.py:117
  (185 shorter events, 125.3 us)
Async XLA Ops:
  22.8 53.4 %all-to-all-start = ((f32[256,19,128]{2,1,0:T(8,128)}), f32[256,19,128]{2,1,0:T(8,128)S(1)}, u32[]{:S(2)}, u32[]{:S(2)}) async-start(f32[256,19,128]{2,1,0:T(8,128)} %scatter_fusion), calls=%async_computation | async-start | bytes 6291456 | tf_op jit(solution)/shard_map/all_to_all | solution.py:65
  179.2 0.7 copy-start.3
  181.0 0.7 copy-start
  181.7 5.9 %collective-permute-start = (f32[17,1,130]{2,1,0:T(1,128)S(1)}, f32[17,1,130]{2,1,0:T(1,128)S(1)}, u32[]{:S(2)}, u32[]{:S(2)}) collective-permute-start(f32[17,1,130]{2,1,0:T(1,128)S(1)} %get-tuple-element.259), channel_id=1, source_target_pairs={{0,8},{8,16},{16,24},{24,32},{32,40},{40,48},{48,56},{56,64},{64,7... | collective-permute-start | bytes 26528 | tf_op jit(solution)/shard_map/ppermute | solution.py:14
  182.7 6.0 %collective-permute-start.1 = (f32[17,1,130]{2,1,0:T(1,128)S(1)}, f32[17,1,130]{2,1,0:T(1,128)S(1)}, u32[]{:S(2)}, u32[]{:S(2)}) collective-permute-start(f32[17,1,130]{2,1,0:T(1,128)S(1)} %get-tuple-element.258), channel_id=1, source_target_pairs={{0,120},{8,0},{16,8},{24,16},{32,24},{40,32},{48,40},{56,48},{64,5... | collective-permute-start | bytes 26528 | tf_op jit(solution)/shard_map/ppermute | solution.py:14
  188.9 3.3 collective-permute-start.2
  190.9 4.0 %collective-permute-start.3 = (f32[17,8,1]{2,1,0:T(8,128)S(1)}, f32[17,8,1]{2,1,0:T(8,128)}, u32[]{:S(2)}, u32[]{:S(2)}) collective-permute-start(f32[17,8,1]{2,1,0:T(8,128)S(1)} %get-tuple-element.260), channel_id=1, source_target_pairs={{0,7},{1,0},{2,1},{3,2},{4,3},{5,4},{6,5},{7,6},{8,15},{9,8},{10,9... | collective-permute-start | bytes 1640 | tf_op jit(solution)/shard_map/ppermute | solution.py:14
  197.2 15.8 %copy-start.1 = (f32[16,8,128]{2,1,0:T(8,128)}, f32[16,8,128]{2,1,0:T(8,128)S(1)}, u32[]{:S(2)}) copy-start(f32[16,8,128]{2,1,0:T(8,128)S(1)} %slice_divide_fusion) | copy-start | bytes 196612
  197.3 6.2 %collective-permute-start.4 = (f32[16,1,128]{2,1,0:T(1,128)S(1)}, f32[16,1,128]{2,1,0:T(1,128)S(1)}, u32[]{:S(2)}, u32[]{:S(2)}) collective-permute-start(f32[16,1,128]{2,1,0:T(1,128)S(1)} %get-tuple-element.264), channel_id=1, source_target_pairs={{0,8},{8,16},{16,24},{24,32},{32,40},{40,48},{48,56},{56,64},{64,7... | collective-permute-start | bytes 24584 | tf_op jit(solution)/shard_map/ppermute | solution.py:24
  197.3 6.1 %collective-permute-start.5 = (f32[16,1,128]{2,1,0:T(1,128)S(1)}, f32[16,1,128]{2,1,0:T(1,128)S(1)}, u32[]{:S(2)}, u32[]{:S(2)}) collective-permute-start(f32[16,1,128]{2,1,0:T(1,128)S(1)} %get-tuple-element.265), channel_id=1, source_target_pairs={{8,0},{16,8},{24,16},{32,24},{40,32},{48,40},{56,48},{64,56},{72,6... | collective-permute-start | bytes 24584 | tf_op jit(solution)/shard_map/ppermute | solution.py:26
  204.2 3.1 collective-permute-start.6
  205.0 4.5 %collective-permute-start.7 = (f32[16,10,1]{2,1,0:T(8,128)S(1)}, f32[16,10,1]{2,1,0:T(8,128)}, u32[]{:S(2)}, u32[]{:S(2)}) collective-permute-start(f32[16,10,1]{2,1,0:T(8,128)S(1)} %get-tuple-element.263), channel_id=1, source_target_pairs={{1,0},{2,1},{3,2},{4,3},{5,4},{6,5},{7,6},{0,7},{9,8},{10,9},{11,1... | collective-permute-start | bytes 1928 | tf_op jit(solution)/shard_map/ppermute | solution.py:26
  207.3 0.7 copy-start.4
  211.4 1.6 copy-start.5
  213.0 107.1 %copy-start.2 = (f32[256,1,128]{2,1,0:T(1,128)S(1)}, f32[256,1,128]{2,1,0:T(1,128)}, u32[]{:S(2)}) copy-start(f32[256,1,128]{2,1,0:T(1,128)} %get-tuple-element.255) | copy-start | bytes 393220
  325.3 41.9 %all-to-all-start.1 = ((f32[256,16,128]{2,1,0:T(8,128)}), f32[256,16,128]{2,1,0:T(8,128)S(1)}, u32[]{:S(2)}, u32[]{:S(2)}) async-start(f32[256,16,128]{2,1,0:T(8,128)} %multiply_add_fusion), calls=%async_computation.1 | async-start | bytes 4194304 | tf_op jit(solution)/shard_map/all_to_all | solution.py:117
where the time goes:
time: 371 us; the launch traced here: 369 us
  matrix products  167 us (45%)
  waiting for transfers between devices  79.5 us (21%)
  local copies, waits for them, and re-layouts  67.9 us (18%)
  starting transfers between devices  37.2 us (10%)
  other arithmetic  15.8 us (4%)
    dot_general x16, matrix products, read_group(): lax.dot_general(mean_flat, onehot, (((1,), (1,)), ((), ())), preferred_el...  84.1 us
    dot_general x16, matrix products, deposit_group(): jnp.dot(rows, onehot, preferred_element_type=jnp.float32, precision=lax.P...  83.1 us
    all_to_all x1, waiting for transfers between devices, per_device(): lax.all_to_all(outgoing, ('wide', 'narrow'), split_axis=0, concat_axis=0,...  41.9 us
    all_to_all x1, waiting for transfers between devices, per_device(): lax.all_to_all(mixed_here, ('wide', 'narrow'), split_axis=0, concat_axis=...  30.5 us
    scatter x1, local copies, waits for them, and re-layouts, per_device(): outgoing = jnp.zeros((slot_total, scalar_count + 3, per_block), jnp.float...  15.6 us
    transpose x16, local copies, waits for them, and re-layouts, deposit_group(): rows = jnp.transpose(piece, (1, 0, 2)).reshape(scalar_count + 1, group_rows)  14.7 us
    all_to_all x1, starting transfers between devices, per_device(): lax.all_to_all(outgoing, ('wide', 'narrow'), split_axis=0, concat_axis=0,...  11.5 us
    all_to_all x1, starting transfers between devices, per_device(): lax.all_to_all(mixed_here, ('wide', 'narrow'), split_axis=0, concat_axis=...  11.4 us
  transfers between devices with their start and end apart: 10, of which 8 were waited for; matrix products, arithmetic and copies ran while one was open for 1% of the time, Pallas kernels for 0%

commit v1 on v0

v1 whole, which is shorter than its diff:
```python
import functools

import jax
import jax.numpy as jnp
from jax import lax
from jax.experimental import pallas as pl
from jax.experimental.pallas import tpu as pltpu
from jax.sharding import PartitionSpec as P

CW = 8
CN = 128
ROWS = CW + 2
COLS = CN + 2
MESH = pl.DeviceIdType.MESH
GROUP = 4


def kernel(
    devices,
    scal_ref,
    mass_ref,
    freq_ref,
    cell_ref,
    owner_ref,
    mixed_ref,
    mean_ref,
    out_buf,
    got_buf,
    near_buf,
    ret_buf,
    left_buf,
    hot_buf,
    acc_ref,
    tile_ref,
    side_buf,
    up_buf,
    side_got,
    diag_got,
    mean_buf,
    idx_vm,
    idx_sm,
    row_buf,
    weight_ref,
    idx_sem,
    send_sem,
    recv_sem,
    back_send,
    back_recv,
    halo_send,
    halo_recv,
):
    f32, bf16 = jnp.float32, jnp.bfloat16
    wide = lax.axis_index("wide")
    narrow = lax.axis_index("narrow")
    me = wide * 8 + narrow
    z, x, y, c = wide // 4, wide % 4, narrow // 2, narrow % 2

    def offsets(k):
        a, b, d, e = k % 4, (k // 4) % 4, (k // 16) % 4, k // 64
        return a, (a + b) % 4, (d + 4 - a) % 4, e

    def ahead(k):
        dz, dx, dy, dc = offsets(k)
        return ((z + dz) % 4) * 4 + (x + dx) % 4, ((y + dy) % 4) * 2 + (c + dc) % 2

    def behind(k):
        dz, dx, dy, dc = offsets(k)
        return (
            ((z + 4 - dz) % 4) * 4 + (x + 4 - dx) % 4,
            ((y + 4 - dy) % 4) * 2 + (c + 2 - dc) % 2,
        )

    lanes = owner_ref.shape[1]
    along = jnp.broadcast_to(owner_ref[...], (lanes, lanes))
    down = along.T
    sub = lax.broadcasted_iota(jnp.int32, (lanes, lanes), 0)
    lane = lax.broadcasted_iota(jnp.int32, (lanes, lanes), 1)
    match = down == lane
    first = jnp.min(jnp.where(match, sub, lanes), axis=0, keepdims=True)
    second = jnp.max(jnp.where(match, sub, -1), axis=0, keepdims=True)
    earlier = jnp.where((down == along) & (sub < lane), 1, 0)
    place = 2 * owner_ref[...] + jnp.max(earlier, axis=0, keepdims=True)
    idx_vm[0:1, :] = jnp.minimum(first, lanes - 1)
    idx_vm[1:2, :] = jnp.maximum(second, 0)
    idx_vm[2:3, :] = first
    idx_vm[3:4, :] = jnp.where(second > first, second, lanes)
    idx_vm[4:5, :] = place
    idx_vm[5:8, :] = jnp.zeros((3, lanes), jnp.int32)
    to_scalar = pltpu.make_async_copy(idx_vm, idx_sm, idx_sem)
    to_scalar.start()
    weight_ref[0:lanes, :] = mass_ref[...]
    weight_ref[lanes : lanes + 8, :] = jnp.zeros((8, CN), f32)
    acc_ref[...] = jnp.zeros_like(acc_ref)
    hot_buf[...] = jnp.zeros_like(hot_buf)
    to_scalar.wait()

    def pack(dest, owner):
        for slot in range(2):
            b = idx_sm[slot, owner]
            m = weight_ref[pl.ds(idx_sm[2 + slot, owner], 1), :]
            dest[16 * slot : 16 * slot + 16, :] = scal_ref[b] * m
            dest[32 + slot : 33 + slot, :] = m
            dest[34 + slot : 35 + slot, :] = cell_ref[pl.ds(b, 1), :].astype(f32)

    def send(k):
        w, v = ahead(k)
        return pltpu.make_async_remote_copy(
            out_buf.at[k],
            got_buf.at[k],
            send_sem,
            recv_sem.at[k],
            device_id=(w, v),
            device_id_type=MESH,
        )

    def send_step(k, carry):
        w, v = ahead(k)
        pack(out_buf.at[k], w * 8 + v)
        send(k).start()
        return carry

    lax.fori_loop(1, devices, send_step, 0)
    pack(got_buf.at[0], me)

    tile_row = lax.broadcasted_iota(jnp.int32, (16, CN), 0).astype(f32)

    def place_of(cells):
        i = jnp.floor((cells + 0.5) * (1.0 / COLS))
        j = cells - i * COLS - 1.0
        return i, jnp.where(j < 0.0, COLS - 1.0, j)

    def fill_hot(j, lane_at):
        j16 = jnp.broadcast_to(j, (16, CN)).astype(bf16)
        for t in range(-(-COLS // 16)):
            hot_buf[16 * t : 16 * t + 16, lane_at : lane_at + CN] = jnp.where(
                (tile_row + 16.0 * t).astype(bf16) == j16, 1.0, 0.0
            ).astype(bf16)

    def deposit(g):
        for n in range(GROUP):
            for slot in range(2):
                at = (2 * n + slot) * CN
                k = g * GROUP + n
                value = got_buf[k, 16 * slot : 16 * slot + 16, :]
                m = got_buf[k, 32 + slot : 33 + slot, :]
                i, j = place_of(got_buf[k, 34 + slot : 35 + slot, :])
                fill_hot(j, at)
                hi = value.astype(bf16)
                lo = (value - hi.astype(f32)).astype(bf16)
                i16 = jnp.broadcast_to(i, (16, CN)).astype(bf16)
                none = jnp.zeros((16, CN), bf16)
                for r in range(ROWS):
                    mask = i16 == jnp.full((16, CN), r, bf16)
                    left_buf[16 * r : 16 * r + 16, at : at + CN] = jnp.where(mask, hi, none)
                    left_buf[160 + 16 * r : 176 + 16 * r, at : at + CN] = jnp.where(mask, lo, none)
                m16 = jnp.broadcast_to(m, (16, CN))
                mhi = m16.astype(bf16)
                mlo = (m16 - mhi.astype(f32)).astype(bf16)
                mask = i16 == tile_row.astype(bf16)
                left_buf[320:336, at : at + CN] = jnp.where(mask, mhi, none)
                left_buf[336:352, at : at + CN] = jnp.where(mask, mlo, none)
        acc_ref[...] += lax.dot_general(
            left_buf[...],
            hot_buf[...],
            (((1,), (1,)), ((), ())),
            preferred_element_type=f32,
        )

    for n in range(1, GROUP):
        send(n).wait_recv()
    deposit(0)

    def deposit_step(g, carry):
        for n in range(GROUP):
            send(g * GROUP + n).wait_recv()
        deposit(g)
        return carry

    lax.fori_loop(1, devices // GROUP, deposit_step, 0)

    tile_ref[0:8, :] = acc_ref[320:328, :] + acc_ref[336:344, :]
    tile_ref[8:168, :] = acc_ref[0:160, :] + acc_ref[160:320, :]
    tile_ref[168:176, :] = acc_ref[328:336, :] + acc_ref[344:352, :]
    own, rest = tile_ref[:, 0:128], tile_ref[:, 128:256]
    at_lane = lax.broadcasted_iota(jnp.int32, (176, 128), 1)
    side_buf[0] = jnp.where(at_lane == 127, pltpu.roll(rest, 126, 1), own)
    side_buf[1] = jnp.where(at_lane == 0, rest, pltpu.roll(own, 2, 1))
    above, below = (wide + 15) % 16, (wide + 1) % 16
    before, after = (narrow + 7) % 8, (narrow + 1) % 8
    top, bottom = pl.ds(0, 40), pl.ds(136, 40)
    halo = [
        (tile_ref.at[top], up_buf.at[1], (above, narrow)),
        (tile_ref.at[bottom], up_buf.at[0], (below, narrow)),
        (side_buf.at[0], side_got.at[1], (wide, before)),
        (side_buf.at[1], side_got.at[0], (wide, after)),
        (side_buf.at[0, top], diag_got.at[3], (above, before)),
        (side_buf.at[0, bottom], diag_got.at[1], (below, before)),
        (side_buf.at[1, top], diag_got.at[2], (above, after)),
        (side_buf.at[1, bottom], diag_got.at[0], (below, after)),
    ]
    halo = [
        pltpu.make_async_remote_copy(
            src, dst, halo_send.at[n], halo_recv.at[n], device_id=to, device_id_type=MESH
        )
        for n, (src, dst, to) in enumerate(halo)
    ]
    for copy in halo:
        copy.start()
    for copy in halo:
        copy.wait()
    nothing = jnp.zeros((96, 128), f32)

    def with_corners(side, high, low):
        return side + jnp.concatenate(
            [high[32:40], high[0:32], nothing, low[8:40], low[0:8]], axis=0
        )

    from_left = with_corners(side_got[0], diag_got[0], diag_got[2])
    from_right = with_corners(side_got[1], diag_got[1], diag_got[3])
    high, low = up_buf[0], up_buf[1]
    nothing2 = jnp.zeros((96, 256), f32)
    vertical = jnp.concatenate(
        [high[32:40], high[0:32], nothing2, low[8:40], low[0:8]], axis=0
    )
    own = (
        own
        + vertical[:, 0:128]
        + jnp.where(at_lane == 0, from_left, 0.0)
        + jnp.where(at_lane == 127, from_right, 0.0)
    )
    rest = (
        rest
        + vertical[:, 128:256]
        + jnp.where(at_lane == 1, from_left, 0.0)
        + jnp.where(at_lane == 0, from_right, 0.0)
    )
    total = jnp.concatenate([own, rest], axis=1)
    for r in range(ROWS):
        at = r if r < 8 else 160 + r
        mean = total[8 + 16 * r : 24 + 16 * r, :] / (total[at : at + 1, :] + 1.0)
        if 1 <= r <= CW:
            mean_ref[:, r - 1, :] = mean[:, 0:CN]
        hi = mean.astype(bf16)
        mean_buf[16 * r : 16 * r + 16, :] = hi
        mean_buf[160 + 16 * r : 176 + 16 * r, :] = (mean - hi.astype(f32)).astype(bf16)

    def lookup(g):
        rows = []
        for n in range(GROUP):
            for slot in range(2):
                k = g * GROUP + n
                i, j = place_of(got_buf[k, 34 + slot : 35 + slot, :])
                fill_hot(j, (2 * n + slot) * CN)
                rows.append(i)
        for n in range(GROUP):
            k = g * GROUP + n
            found = jnp.dot(
                mean_buf[...],
                hot_buf[:, 256 * n : 256 * n + 256],
                preferred_element_type=f32,
            )
            for slot in range(2):
                i16 = jnp.broadcast_to(rows[2 * n + slot], (16, CN))
                near = jnp.zeros((16, CN), f32)
                cut = slice(CN * slot, CN * slot + CN)
                for r in range(ROWS):
                    near = near + jnp.where(
                        i16 == float(r),
                        found[16 * r : 16 * r + 16, cut] + found[160 + 16 * r : 176 + 16 * r, cut],
                        0.0,
                    )
                near_buf[2 * k + slot] = near

    def give_back(k):
        w, v = behind(k)
        return pltpu.make_async_remote_copy(
            near_buf.at[pl.ds(2 * k, 2)],
            ret_buf.at[pl.ds(2 * me, 2)],
            back_send,
            back_recv.at[k],
            device_id=(w, v),
            device_id_type=MESH,
        )

    def take_back(k):
        w, v = ahead(k)
        return pltpu.make_async_remote_copy(
            near_buf.at[pl.ds(2 * k, 2)],
            ret_buf.at[pl.ds(2 * (w * 8 + v), 2)],
            back_send,
            back_recv.at[k],
            device_id=(w, v),
            device_id_type=MESH,
        )

    lookup(0)
    ret_buf[pl.ds(2 * me, 2)] = near_buf[0:2]
    for n in range(1, GROUP):
        give_back(n).start()

    def lookup_step(g, carry):
        lookup(g)
        for n in range(GROUP):
            give_back(g * GROUP + n).start()
        return carry

    lax.fori_loop(1, devices // GROUP, lookup_step, 0)

    def arrive(k, carry):
        take_back(k).wait_recv()
        return carry

    lax.fori_loop(1, devices, arrive, 0)

    def read_rate(b, carry):
        p = idx_sm[4, b]
        row_buf[pl.ds(b, 1), :] = ret_buf[p, 0:1, :]
        return carry

    lax.fori_loop(0, lanes, read_rate, 0, unroll=4)
    row_buf[...] = jnp.exp(-freq_ref[...] * (1.5 + jnp.tanh(row_buf[...])))

    def mix(b, carry):
        p = idx_sm[4, b]
        near = ret_buf[p]
        mixed_ref[b] = near + (scal_ref[b] - near) * row_buf[pl.ds(b, 1), :]
        return carry

    lax.fori_loop(0, lanes, mix, 0, unroll=4)

    rest_of = pl.ds(1, devices - 1)
    pltpu.make_async_copy(out_buf.at[rest_of], got_buf.at[rest_of], send_sem).wait()
    rest_of = pl.ds(2, 2 * (devices - 1))
    pltpu.make_async_copy(near_buf.at[rest_of], ret_buf.at[rest_of], back_send).wait()


def per_device(scalars, mass, frequency, cell, owner):
    devices = lax.axis_size("wide") * lax.axis_size("narrow")
    blocks, count, per_block = scalars.shape
    f32, bf16 = jnp.float32, jnp.bfloat16
    vmem = pl.BlockSpec(memory_space=pltpu.VMEM)
    return pl.pallas_call(
        functools.partial(kernel, devices),
        out_shape=(
            jax.ShapeDtypeStruct((blocks, count, per_block), f32),
            jax.ShapeDtypeStruct((count, CW, CN), f32),
        ),
        in_specs=[vmem] * 5,
        out_specs=(vmem, vmem),
        scratch_shapes=[
            pltpu.VMEM((devices, 36, per_block), f32),
            pltpu.VMEM((devices, 36, per_block), f32),
            pltpu.VMEM((2 * devices, 16, per_block), f32),
            pltpu.VMEM((2 * devices, 16, per_block), f32),
            pltpu.VMEM((352, GROUP * 256), bf16),
            pltpu.VMEM((256, GROUP * 256), bf16),
            pltpu.VMEM((352, 256), f32),
            pltpu.VMEM((176, 256), f32),
            pltpu.VMEM((2, 176, 128), f32),
            pltpu.VMEM((2, 40, 256), f32),
            pltpu.VMEM((2, 176, 128), f32),
            pltpu.VMEM((4, 40, 128), f32),
            pltpu.VMEM((320, 256), bf16),
            pltpu.VMEM((8, blocks), jnp.int32),
            pltpu.SMEM((8, blocks), jnp.int32),
            pltpu.VMEM((blocks, per_block), f32),
            pltpu.VMEM((blocks + 8, per_block), f32),
            pltpu.SemaphoreType.DMA,
            pltpu.SemaphoreType.DMA,
            pltpu.SemaphoreType.DMA((devices,)),
            pltpu.SemaphoreType.DMA,
            pltpu.SemaphoreType.DMA((devices,)),
            pltpu.SemaphoreType.DMA((8,)),
            pltpu.SemaphoreType.DMA((8,)),
        ],
        compiler_params=pltpu.CompilerParams(
            has_side_effects=True, vmem_limit_bytes=48 << 20
        ),
        name="mixing",
    )(scalars, mass, frequency, cell, owner.reshape(1, blocks))


def solution(mesh):
    held = P(("wide", "narrow"), None)
    block = P(("wide", "narrow"), None, None)
    return jax.shard_map(
        per_device,
        mesh=mesh,
        in_specs=(block, held, held, held, held),
        out_specs=(block, P(None, "wide", "narrow")),
        check_vma=False,
    )
```

time: 371 us -> 93.6 us (0.25)
  matrix products: 167 us -> 0 us
  Pallas kernels: 0 us -> 86.7 us
  waiting for transfers between devices: 79.5 us -> 0 us
  local copies, waits for them, and re-layouts: 67.9 us -> 5.99 us
  starting transfers between devices: 37.2 us -> 0 us
  other arithmetic: 15.8 us -> 0 us
    dot_general x32 -> x0, matrix products: 167 us -> none  [the longest x16 84.1 us: read_group(): lax.dot_general(mean_flat, onehot, (((1,), (1,)), ((), ())), preferred_el...]
    pallas_call x0 -> x1, Pallas kernels: none -> 86.7 us  [per_device(): pl.pallas_call(functools.partial(kernel, devices), out_shape=(jax.ShapeDt...]
    all_to_all x2 -> x0, waiting for transfers between devices: 72.4 us -> none  [the longest x1 41.9 us: per_device(): lax.all_to_all(outgoing, ('wide', 'narrow'), split_axis=0, concat_axis=0,...]
    all_to_all x2 -> x0, starting transfers between devices: 22.9 us -> none  [the longest x1 11.5 us: per_device(): lax.all_to_all(outgoing, ('wide', 'narrow'), split_axis=0, concat_axis=0,...]
    scatter x1 -> x0, local copies, waits for them, and re-layouts: 15.6 us -> none  [per_device(): outgoing = jnp.zeros((slot_total, scalar_count + 3, per_block), jnp.float...]
    transpose x16 -> x0, local copies, waits for them, and re-layouts: 14.7 us -> none  [deposit_group(): rows = jnp.transpose(piece, (1, 0, 2)).reshape(scalar_count + 1, group_rows)]
    ppermute x8 -> x0, starting transfers between devices: 14.3 us -> none  [the longest x4 6.86 us: shifted(): lax.ppermute(shard, axis, [(i, (i + by) % length) for i in range(length)])]
    eq x32 -> x0, local copies, waits for them, and re-layouts: 11.4 us -> none  [table_for(): cells[:, None] == jnp.arange(extent, dtype=jnp.int32)[None, :]]
  transfers between devices with their start and end apart: 10 -> 0, of which waited for: 8 -> 0; matrix products, arithmetic and copies ran while one was open for 1% -> 0% of each run, Pallas kernels for 0% -> 0%
where the time goes in v1:
time: 93.6 us; the launch traced here: 93.3 us
  Pallas kernels  86.7 us (93%)
  local copies, waits for them, and re-layouts  5.99 us (6%)
    pallas_call x1, Pallas kernels, per_device(): pl.pallas_call(functools.partial(kernel, devices), out_shape=(jax.ShapeDt...  86.7 us
    unnamed x12, local copies, waits for them, and re-layouts  5.99 us

profile of v1, /device:TPU:1, one launch (start us, length us, event | category | flops | bytes accessed | tf_op | source)
XLA Modules:
  0.0 93.3 jit_solution(14940154770342885364)
XLA Ops:
  0.6 0.0 copy-start.4
  0.6 0.6 copy-done.4
  1.3 0.0 copy-start
  1.3 1.2 %copy-done = f32[128,16,128]{2,1,0:T(8,128)S(1)} copy-done((f32[128,16,128]{2,1,0:T(8,128)S(1)}, f32[128,16,128]{2,1,0:T(8,128)}, u32[]{:S(2)}) %copy-start) | copy-done | bytes 1048600
  2.5 0.0 copy-start.1
  2.5 0.8 copy-done.1
  3.4 0.0 copy-start.2
  3.4 0.8 copy-done.2
  4.2 0.0 copy-start.3
  4.2 0.8 copy-done.3
  5.0 86.7 %mixing.1 = (f32[128,16,128]{2,1,0:T(8,128)S(1)}, f32[16,8,128]{2,1,0:T(8,128)S(1)}) custom-call(f32[128,16,128]{2,1,0:T(8,128)S(1)} %copy-done, f32[128,128]{1,0:T(8,128)S(1)} %copy-done.1, f32[128,128]{1,0:T(8,128)S(1)} %copy-done.2, s32[128,128]{1,0:T(8,128)S(1)} %copy-done.3, s32[1,128]{1,0:T(1,128)S(1)} %bitcast.1), custom_call_target="tpu_custom_call" | custom-call | tf_op jit(solution)/shard_map/mixing/pallas_call | solution.py:342
  91.7 1.0 %copy.9 = f32[128,16,128]{2,1,0:T(8,128)} copy(f32[128,16,128]{2,1,0:T(8,128)S(1)} %get-tuple-element.4) | data formatting | bytes 2097152
  92.7 0.6 copy.10
Async XLA Ops:
  0.6 0.7 copy-start.4
  1.3 1.2 %copy-start = (f32[128,16,128]{2,1,0:T(8,128)S(1)}, f32[128,16,128]{2,1,0:T(8,128)}, u32[]{:S(2)}) copy-start(f32[128,16,128]{2,1,0:T(8,128)} %scal_ref.1) | copy-start | bytes 3145732
  2.5 0.8 copy-start.1
  3.4 0.8 copy-start.2
  4.2 0.8 copy-start.3

commit v2 on v1

--- a/solution.py
+++ b/solution.py
@@ -17,19 +17,25 @@
 
 def kernel(
     devices,
-    scal_ref,
-    mass_ref,
-    freq_ref,
-    cell_ref,
-    owner_ref,
+    scal_hbm,
+    mass_hbm,
+    freq_hbm,
+    cell_hbm,
+    owner_hbm,
     mixed_ref,
     mean_ref,
     out_buf,
     got_buf,
     near_buf,
     ret_buf,
-    left_buf,
-    hot_buf,
+    scal_ref,
+    freq_ref,
+    cell_ref,
+    owner_ref,
+    left_even,
+    left_odd,
+    hot_even,
+    hot_odd,
     acc_ref,
     tile_ref,
     side_buf,
@@ -41,6 +47,8 @@
     idx_sm,
     row_buf,
     weight_ref,
+    load_sem,
+    hello_sem,
     idx_sem,
     send_sem,
     recv_sem,
@@ -50,27 +58,65 @@
     halo_recv,
 ):
     f32, bf16 = jnp.float32, jnp.bfloat16
+    left_bufs, hot_bufs = (left_even, left_odd), (hot_even, hot_odd)
     wide = lax.axis_index("wide")
     narrow = lax.axis_index("narrow")
     me = wide * 8 + narrow
-    z, x, y, c = wide // 4, wide % 4, narrow // 2, narrow % 2
-
-    def offsets(k):
-        a, b, d, e = k % 4, (k // 4) % 4, (k // 16) % 4, k // 64
-        return a, (a + b) % 4, (d + 4 - a) % 4, e
-
-    def ahead(k):
-        dz, dx, dy, dc = offsets(k)
-        return ((z + dz) % 4) * 4 + (x + dx) % 4, ((y + dy) % 4) * 2 + (c + dc) % 2
-
-    def behind(k):
-        dz, dx, dy, dc = offsets(k)
-        return (
-            ((z + 4 - dz) % 4) * 4 + (x + 4 - dx) % 4,
-            ((y + 4 - dy) % 4) * 2 + (c + 2 - dc) % 2,
+    here = (lax.div(wide, 4), lax.rem(wide, 4), lax.div(narrow, 2), lax.rem(narrow, 2))
+
+    def at_offset(offset, sign=1):
+        z, x, y, c = (
+            lax.rem(h + (d if sign > 0 else n - d), n) for h, d, n in zip(here, offset, (4, 4, 4, 2))
         )
+        return z * 4 + x, y * 2 + c
+
+    near_by = [(0, 0, 0, 1)]
+    for d in (1, 3, 2):
+        near_by += [(d, 0, 0, 0), (0, d, 0, 0), (0, 0, d, 0)]
+
+    def two_axes(i):
+        a, b = 1 + lax.div(i, 3), 1 + lax.rem(i, 3)
+        on = [1 - lax.div(lax.rem(b - 1 + n, 3) + 1, 2) for n in (0, 2, 1)]
+        return [(a, b, 0, 0), (b, 0, a, 0), (0, a, b, 0), (on[0] * a, on[1] * a, on[2] * a, 1)]
+
+    def three_axes(i):
+        a, b = 1 + lax.div(i, 3), 1 + lax.rem(i, 3)
+        last = [(a, b, n, 0) for n in (1, 2, 3)]
+        return [last[0], (a, b, 0, 1), last[1], (b, 0, a, 1), last[2], (0, a, b, 1)]
+
+    def four_axes(i):
+        a, b = 1 + lax.div(i, 3), 1 + lax.rem(i, 3)
+        return [(a, b, n, 1) for n in (1, 2, 3)]
+
+    classes = [(11, 9, two_axes), (47, 9, three_axes), (101, 9, four_axes)]
+
+    def hello(sem):
+        for offset in near_by:
+            pl.semaphore_signal(sem, inc=1, device_id=at_offset(offset), device_id_type=MESH)
+
+    barrier = pltpu.get_barrier_semaphore()
+    hello(barrier)
+    loads = [
+        pltpu.make_async_copy(src, dst, load_sem.at[n])
+        for n, (src, dst) in enumerate(
+            (
+                (owner_hbm, owner_ref),
+                (scal_hbm, scal_ref),
+                (mass_hbm, weight_ref.at[pl.ds(0, mass_hbm.shape[0])]),
+                (cell_hbm, cell_ref),
+                (freq_hbm, freq_ref),
+            )
+        )
+    ]
+    for copy in loads:
+        copy.start()
 
     lanes = owner_ref.shape[1]
+    weight_ref[lanes : lanes + 8, :] = jnp.zeros((8, CN), f32)
+    acc_ref[...] = jnp.zeros_like(acc_ref)
+    for hot_buf in hot_bufs:
+        hot_buf[144:256, :] = jnp.zeros((112, hot_buf.shape[1]), bf16)
+    loads[0].wait()
     along = jnp.broadcast_to(owner_ref[...], (lanes, lanes))
     down = along.T
     sub = lax.broadcasted_iota(jnp.int32, (lanes, lanes), 0)
@@ -88,11 +134,9 @@
     idx_vm[5:8, :] = jnp.zeros((3, lanes), jnp.int32)
     to_scalar = pltpu.make_async_copy(idx_vm, idx_sm, idx_sem)
     to_scalar.start()
-    weight_ref[0:lanes, :] = mass_ref[...]
-    weight_ref[lanes : lanes + 8, :] = jnp.zeros((8, CN), f32)
-    acc_ref[...] = jnp.zeros_like(acc_ref)
-    hot_buf[...] = jnp.zeros_like(hot_buf)
     to_scalar.wait()
+    for copy in loads[1:]:
+        copy.wait()
 
     def pack(dest, owner):
         for slot in range(2):
@@ -102,41 +146,58 @@
             dest[32 + slot : 33 + slot, :] = m
             dest[34 + slot : 35 + slot, :] = cell_ref[pl.ds(b, 1), :].astype(f32)
 
-    def send(k):
-        w, v = ahead(k)
-        return pltpu.make_async_remote_copy(
-            out_buf.at[k],
-            got_buf.at[k],
+    def send_to(p, offset):
+        w, v = at_offset(offset)
+        pack(out_buf.at[p], w * 8 + v)
+        pltpu.make_async_remote_copy(
+            out_buf.at[p],
+            got_buf.at[p],
             send_sem,
-            recv_sem.at[k],
+            recv_sem.at[p],
             device_id=(w, v),
             device_id_type=MESH,
-        )
-
-    def send_step(k, carry):
-        w, v = ahead(k)
-        pack(out_buf.at[k], w * 8 + v)
-        send(k).start()
-        return carry
-
-    lax.fori_loop(1, devices, send_step, 0)
+        ).start()
+
+    def send_class(base, steps, offsets):
+        def body(i, carry):
+            listed = offsets(i)
+            for n, offset in enumerate(listed):
+                send_to(base + len(listed) * i + n, offset)
+            return carry
+
+        lax.fori_loop(0, steps, body, 0)
+
+    pl.semaphore_wait(barrier, len(near_by))
+    hello(hello_sem.at[0])
+    for n, offset in enumerate(near_by):
+        send_to(1 + n, offset)
+    pl.semaphore_wait(hello_sem.at[0], len(near_by))
+    hello(hello_sem.at[1])
+    send_class(*classes[0])
+    pl.semaphore_wait(hello_sem.at[1], len(near_by))
+    hello(hello_sem.at[2])
+    send_class(*classes[1])
+    pl.semaphore_wait(hello_sem.at[2], len(near_by))
+    send_class(*classes[2])
     pack(got_buf.at[0], me)
 
     tile_row = lax.broadcasted_iota(jnp.int32, (16, CN), 0).astype(f32)
+    row16 = tile_row.astype(bf16)
+    none, one = jnp.zeros((16, CN), bf16), jnp.ones((16, CN), bf16)
 
     def place_of(cells):
         i = jnp.floor((cells + 0.5) * (1.0 / COLS))
         j = cells - i * COLS - 1.0
         return i, jnp.where(j < 0.0, COLS - 1.0, j)
 
-    def fill_hot(j, lane_at):
+    def fill_hot(hot_buf, j, lane_at):
         j16 = jnp.broadcast_to(j, (16, CN)).astype(bf16)
         for t in range(-(-COLS // 16)):
             hot_buf[16 * t : 16 * t + 16, lane_at : lane_at + CN] = jnp.where(
-                (tile_row + 16.0 * t).astype(bf16) == j16, 1.0, 0.0
-            ).astype(bf16)
-
-    def deposit(g):
+                row16 + jnp.full((16, CN), 16 * t, bf16) == j16, one, none
+            )
+
+    def build(g, left_buf, hot_buf):
         for n in range(GROUP):
             for slot in range(2):
                 at = (2 * n + slot) * CN
@@ -144,11 +205,10 @@
                 value = got_buf[k, 16 * slot : 16 * slot + 16, :]
                 m = got_buf[k, 32 + slot : 33 + slot, :]
                 i, j = place_of(got_buf[k, 34 + slot : 35 + slot, :])
-                fill_hot(j, at)
+                fill_hot(hot_buf, j, at)
                 hi = value.astype(bf16)
                 lo = (value - hi.astype(f32)).astype(bf16)
                 i16 = jnp.broadcast_to(i, (16, CN)).astype(bf16)
-                none = jnp.zeros((16, CN), bf16)
                 for r in range(ROWS):
                     mask = i16 == jnp.full((16, CN), r, bf16)
                     left_buf[16 * r : 16 * r + 16, at : at + CN] = jnp.where(mask, hi, none)
@@ -156,9 +216,11 @@
                 m16 = jnp.broadcast_to(m, (16, CN))
                 mhi = m16.astype(bf16)
                 mlo = (m16 - mhi.astype(f32)).astype(bf16)
-                mask = i16 == tile_row.astype(bf16)
+                mask = i16 == row16
                 left_buf[320:336, at : at + CN] = jnp.where(mask, mhi, none)
                 left_buf[336:352, at : at + CN] = jnp.where(mask, mlo, none)
+
+    def add_up(left_buf, hot_buf):
         acc_ref[...] += lax.dot_general(
             left_buf[...],
             hot_buf[...],
@@ -166,17 +228,38 @@
             preferred_element_type=f32,
         )
 
-    for n in range(1, GROUP):
-        send(n).wait_recv()
-    deposit(0)
-
-    def deposit_step(g, carry):
-        for n in range(GROUP):
-            send(g * GROUP + n).wait_recv()
-        deposit(g)
+    def wait_for(g, skip=0):
+        for n in range(skip, GROUP):
+            p = g * GROUP + n
+            pltpu.make_async_copy(out_buf.at[p], got_buf.at[p], recv_sem.at[p]).wait()
+
+    even, odd = (left_bufs[0], hot_bufs[0]), (left_bufs[1], hot_bufs[1])
+    groups = devices // GROUP
+
+    def deposit_step(t, carry):
+        wait_for(2 * t + 1)
+        add_up(*even)
+        build(2 * t + 1, *odd)
+        wait_for(2 * t + 2)
+        add_up(*odd)
+        build(2 * t + 2, *even)
         return carry
 
-    lax.fori_loop(1, devices // GROUP, deposit_step, 0)
+    wait_for(0,1)
+    wait_for(1)
+    build(0,*even)
+    build(1,*odd)
+    add_up(*even)
+    add_up(*odd)
+    def ds(t,carry):
+        wait_for(2 * t)
+        wait_for(2 * t + 1)
+        build(2*t,*even)
+        build(2*t+1,*odd)
+        add_up(*even)
+        add_up(*odd)
+        return carry
+    lax.fori_loop(1, groups // 2, ds, 0)
 
     tile_ref[0:8, :] = acc_ref[320:328, :] + acc_ref[336:344, :]
     tile_ref[8:168, :] = acc_ref[0:160, :] + acc_ref[160:320, :]
@@ -244,16 +327,14 @@
         mean_buf[16 * r : 16 * r + 16, :] = hi
         mean_buf[160 + 16 * r : 176 + 16 * r, :] = (mean - hi.astype(f32)).astype(bf16)
 
-    def lookup(g):
+    def lookup(p, count, hot_buf):
         rows = []
-        for n in range(GROUP):
+        for n in range(count):
             for slot in range(2):
-                k = g * GROUP + n
-                i, j = place_of(got_buf[k, 34 + slot : 35 + slot, :])
-                fill_hot(j, (2 * n + slot) * CN)
+                i, j = place_of(got_buf[p + n, 34 + slot : 35 + slot, :])
+                fill_hot(hot_buf, j, (2 * n + slot) * CN)
                 rows.append(i)
-        for n in range(GROUP):
-            k = g * GROUP + n
+        for n in range(count):
             found = jnp.dot(
                 mean_buf[...],
                 hot_buf[:, 256 * n : 256 * n + 256],
@@ -269,45 +350,43 @@
                         found[16 * r : 16 * r + 16, cut] + found[160 + 16 * r : 176 + 16 * r, cut],
                         0.0,
                     )
-                near_buf[2 * k + slot] = near
-
-    def give_back(k):
-        w, v = behind(k)
-        return pltpu.make_async_remote_copy(
-            near_buf.at[pl.ds(2 * k, 2)],
+                near_buf[2 * (p + n) + slot] = near
+
+    def give_back(p, offset):
+        pltpu.make_async_remote_copy(
+            near_buf.at[pl.ds(2 * p, 2)],
             ret_buf.at[pl.ds(2 * me, 2)],
             back_send,
-            back_recv.at[k],
-            device_id=(w, v),
+            back_recv.at[p],
+            device_id=at_offset(offset, -1),
             device_id_type=MESH,
-        )
-
-    def take_back(k):
-        w, v = ahead(k)
-        return pltpu.make_async_remote_copy(
-            near_buf.at[pl.ds(2 * k, 2)],
-            ret_buf.at[pl.ds(2 * (w * 8 + v), 2)],
-            back_send,
-            back_recv.at[k],
-            device_id=(w, v),
-            device_id_type=MESH,
-        )
-
-    lookup(0)
+        ).start()
+
+    def return_class(base, steps, offsets):
+        def body(i, carry):
+            listed = offsets(i)
+            p = base + len(listed) * i
+            for n in range(0, len(listed), 3):
+                some = listed[n : n + 3]
+                lookup(p + n, len(some), hot_bufs[(n // 3) % 2])
+                for m, offset in enumerate(some):
+                    give_back(p + n + m, offset)
+            return carry
+
+        lax.fori_loop(0, steps, body, 0)
+
+    for arguments in reversed(classes):
+        return_class(*arguments)
+    for p in (8, 4, 0):
+        lookup(p, min(4, 11 - p), hot_bufs[(p // 4) % 2])
+        for n in range(p, min(p + 4, 11)):
+            if n:
+                give_back(n, near_by[n - 1])
     ret_buf[pl.ds(2 * me, 2)] = near_buf[0:2]
-    for n in range(1, GROUP):
-        give_back(n).start()
-
-    def lookup_step(g, carry):
-        lookup(g)
-        for n in range(GROUP):
-            give_back(g * GROUP + n).start()
-        return carry
-
-    lax.fori_loop(1, devices // GROUP, lookup_step, 0)
-
-    def arrive(k, carry):
-        take_back(k).wait_recv()
+
+    def arrive(p, carry):
+        pair = pl.ds(2 * p, 2)
+        pltpu.make_async_copy(near_buf.at[pair], ret_buf.at[pair], back_recv.at[p]).wait()
         return carry
 
     lax.fori_loop(1, devices, arrive, 0)
@@ -345,14 +424,20 @@
             jax.ShapeDtypeStruct((blocks, count, per_block), f32),
             jax.ShapeDtypeStruct((count, CW, CN), f32),
         ),
-        in_specs=[vmem] * 5,
+        in_specs=[pl.BlockSpec(memory_space=pltpu.HBM)] * 5,
         out_specs=(vmem, vmem),
         scratch_shapes=[
             pltpu.VMEM((devices, 36, per_block), f32),
             pltpu.VMEM((devices, 36, per_block), f32),
             pltpu.VMEM((2 * devices, 16, per_block), f32),
             pltpu.VMEM((2 * devices, 16, per_block), f32),
+            pltpu.VMEM((blocks, count, per_block), f32),
+            pltpu.VMEM((blocks, per_block), f32),
+            pltpu.VMEM((blocks, per_block), jnp.int32),
+            pltpu.VMEM((1, blocks), jnp.int32),
             pltpu.VMEM((352, GROUP * 256), bf16),
+            pltpu.VMEM((352, GROUP * 256), bf16),
+            pltpu.VMEM((256, GROUP * 256), bf16),
             pltpu.VMEM((256, GROUP * 256), bf16),
             pltpu.VMEM((352, 256), f32),
             pltpu.VMEM((176, 256), f32),
@@ -365,6 +450,8 @@
             pltpu.SMEM((8, blocks), jnp.int32),
             pltpu.VMEM((blocks, per_block), f32),
             pltpu.VMEM((blocks + 8, per_block), f32),
+            pltpu.SemaphoreType.DMA((5,)),
+            pltpu.SemaphoreType.REGULAR((3,)),
             pltpu.SemaphoreType.DMA,
             pltpu.SemaphoreType.DMA,
             pltpu.SemaphoreType.DMA((devices,)),
@@ -374,7 +461,7 @@
             pltpu.SemaphoreType.DMA((8,)),
         ],
         compiler_params=pltpu.CompilerParams(
-            has_side_effects=True, vmem_limit_bytes=48 << 20
+            collective_id=0, has_side_effects=True, vmem_limit_bytes=64 << 20
         ),
         name="mixing",
     )(scalars, mass, frequency, cell, owner.reshape(1, blocks))

time: 93.6 us -> 82.2 us (0.88)
  Pallas kernels: 86.7 us -> 78.5 us
  local copies, waits for them, and re-layouts: 5.99 us -> 2.93 us
    pallas_call x1, Pallas kernels: 86.7 us -> 78.5 us  [per_device(): pl.pallas_call(functools.partial(kernel, devices), out_shape=(jax.ShapeDt...]
    unnamed x12 -> x4, local copies, waits for them, and re-layouts: 5.99 us -> 2.93 us
where the time goes in v2:
time: 82.2 us; the launch traced here: 82.1 us
  Pallas kernels  78.5 us (95%)
  local copies, waits for them, and re-layouts  2.93 us (4%)
    pallas_call x1, Pallas kernels, per_device(): pl.pallas_call(functools.partial(kernel, devices), out_shape=(jax.ShapeDt...  78.5 us
    unnamed x4, local copies, waits for them, and re-layouts  2.93 us

profile of v2, /device:TPU:1, one launch (start us, length us, event | category | flops | bytes accessed | tf_op | source)
XLA Modules:
  0.0 82.1 jit_solution(9397545966135164624)
XLA Ops:
  0.6 78.5 %mixing.1 = (f32[128,16,128]{2,1,0:T(8,128)}, f32[16,8,128]{2,1,0:T(8,128)}) custom-call(f32[128,16,128]{2,1,0:T(8,128)} %scal_hbm.1, f32[128,128]{1,0:T(8,128)} %mass_hbm.1, f32[128,128]{1,0:T(8,128)} %freq_hbm.1, s32[128,128]{1,0:T(8,128)} %cell_hbm.1, s32[1,128]{1,0:T(1,128)} %bitcast.1), custom_call_target="tpu_custom_call" | custom-call | tf_op jit(solution)/shard_map/mixing/pallas_call | solution.py:421
  79.2 0.0 copy-start
  79.2 2.3 %copy.9 = f32[128,16,128]{2,1,0:T(8,128)} copy(f32[128,16,128]{2,1,0:T(8,128)} %get-tuple-element.4) | data formatting | bytes 2097152
  81.5 0.0 copy-done
  81.5 0.6 copy.10
Async XLA Ops:
  79.2 2.3 %copy-start = (f32[16,8,128]{2,1,0:T(8,128)S(1)}, f32[16,8,128]{2,1,0:T(8,128)}, u32[]{:S(2)}) copy-start(f32[16,8,128]{2,1,0:T(8,128)} %get-tuple-element.5) | copy-start | bytes 196612

commit v3 on v2

v3 whole, which is shorter than its diff:
```python
import functools

import jax
import jax.numpy as jnp
from jax import lax
from jax.experimental import pallas as pl
from jax.experimental.pallas import tpu as pltpu
from jax.sharding import PartitionSpec as P

CW = 8
CN = 128
ROWS = CW + 2
COLS = CN + 2
MESH = pl.DeviceIdType.MESH
GROUP = 4
PAIR = 2 * GROUP
EARLY = 14


def kernel(
    devices,
    scal_hbm,
    mass_hbm,
    freq_hbm,
    cell_hbm,
    owner_hbm,
    mixed_ref,
    mean_ref,
    out_a,
    out_b,
    got_a,
    got_b,
    near_a,
    near_b,
    ret_a,
    ret_b,
    scal_ref,
    freq_ref,
    cell_ref,
    owner_ref,
    left_even,
    left_odd,
    hot_even,
    hot_odd,
    acc_a,
    acc_b,
    tile_a,
    tile_b,
    side_a,
    side_b,
    up_a,
    up_b,
    side_got_a,
    side_got_b,
    diag_a,
    diag_b,
    mean_a,
    mean_b,
    inverse_ref,
    idx_vm,
    idx_sm,
    row_buf,
    weight_ref,
    load_sem,
    hello_sem,
    idx_sem,
    send_sem,
    recv_sem,
    back_send,
    back_recv,
    halo_send,
    halo_recv,
):
    f32, bf16 = jnp.float32, jnp.bfloat16
    wide = lax.axis_index("wide")
    narrow = lax.axis_index("narrow")
    me = wide * 8 + narrow
    here = (lax.div(wide, 4), lax.rem(wide, 4), lax.div(narrow, 2), lax.rem(narrow, 2))

    def at_offset(offset, sign=1):
        z, x, y, c = (
            lax.rem(h + (d if sign > 0 else n - d), n) for h, d, n in zip(here, offset, (4, 4, 4, 2))
        )
        return z * 4 + x, y * 2 + c

    near_by = [(0, 0, 0, 1)]
    for d in (1, 3, 2):
        near_by += [(d, 0, 0, 0), (0, d, 0, 0), (0, 0, d, 0)]

    def two_axes(i):
        a, b = 1 + lax.div(i, 3), 1 + lax.rem(i, 3)
        on = [1 - lax.div(lax.rem(b - 1 + n, 3) + 1, 2) for n in (0, 2, 1)]
        return [(a, b, 0, 0), (b, 0, a, 0), (0, a, b, 0), (on[0] * a, on[1] * a, on[2] * a, 1)]

    def three_axes(i):
        a, b = 1 + lax.div(i, 3), 1 + lax.rem(i, 3)
        last = [(a, b, n, 0) for n in (1, 2, 3)]
        return [last[0], (a, b, 0, 1), last[1], (b, 0, a, 1), last[2], (0, a, b, 1)]

    def four_axes(i):
        a, b = 1 + lax.div(i, 3), 1 + lax.rem(i, 3)
        return [(a, b, n, 1) for n in (1, 2, 3)]

    classes = [(11, 9, two_axes), (47, 9, three_axes), (101, 9, four_axes)]

    def hello(sem):
        for offset in near_by:
            pl.semaphore_signal(sem, inc=1, device_id=at_offset(offset), device_id_type=MESH)

    barrier = pltpu.get_barrier_semaphore()
    hello(barrier)
    loads = [
        pltpu.make_async_copy(src, dst, load_sem.at[n])
        for n, (src, dst) in enumerate(
            (
                (owner_hbm, owner_ref),
                (scal_hbm, scal_ref),
                (mass_hbm, weight_ref.at[pl.ds(0, mass_hbm.shape[0])]),
                (cell_hbm, cell_ref),
                (freq_hbm, freq_ref),
            )
        )
    ]
    for copy in loads:
        copy.start()

    lanes = owner_ref.shape[1]
    weight_ref[lanes : lanes + 8, :] = jnp.zeros((8, CN), f32)
    acc_a[...] = jnp.zeros_like(acc_a)
    acc_b[...] = jnp.zeros_like(acc_b)
    for hot_buf in (hot_even, hot_odd):
        hot_buf[144:256, :] = jnp.zeros((112, hot_buf.shape[1]), bf16)
    loads[0].wait()
    along = jnp.broadcast_to(owner_ref[...], (lanes, lanes))
    down = along.T
    sub = lax.broadcasted_iota(jnp.int32, (lanes, lanes), 0)
    lane = lax.broadcasted_iota(jnp.int32, (lanes, lanes), 1)
    match = down == lane
    first = jnp.min(jnp.where(match, sub, lanes), axis=0, keepdims=True)
    second = jnp.max(jnp.where(match, sub, -1), axis=0, keepdims=True)
    earlier = jnp.where((down == along) & (sub < lane), 1, 0)
    place = 2 * owner_ref[...] + jnp.max(earlier, axis=0, keepdims=True)
    idx_vm[0:1, :] = jnp.minimum(first, lanes - 1)
    idx_vm[1:2, :] = jnp.maximum(second, 0)
    idx_vm[2:3, :] = first
    idx_vm[3:4, :] = jnp.where(second > first, second, lanes)
    idx_vm[4:5, :] = place
    idx_vm[5:8, :] = jnp.zeros((3, lanes), jnp.int32)
    to_scalar = pltpu.make_async_copy(idx_vm, idx_sm, idx_sem)
    to_scalar.start()
    to_scalar.wait()
    for copy in loads[1:]:
        copy.wait()

    outs, gots = (out_a, out_b), (got_a, got_b)
    nears, rets = (near_a, near_b), (ret_a, ret_b)
    accs, tiles, means = (acc_a, acc_b), (tile_a, tile_b), (mean_a, mean_b)

    def pack(half, dest, owner):
        for slot in range(2):
            b = idx_sm[slot, owner]
            m = weight_ref[pl.ds(idx_sm[2 + slot, owner], 1), :]
            dest[8 * slot : 8 * slot + 8, :] = scal_ref[b, 8 * half : 8 * half + 8, :] * m
            if half == 0:
                dest[16 + slot : 17 + slot, :] = m
                dest[18 + slot : 19 + slot, :] = cell_ref[pl.ds(b, 1), :].astype(f32)

    def send_to(half, p, offset):
        w, v = at_offset(offset)
        pack(half, outs[half].at[p], w * 8 + v)
        pltpu.make_async_remote_copy(
            outs[half].at[p],
            gots[half].at[p],
            send_sem.at[half],
            recv_sem.at[half, lax.div(p, PAIR)],
            device_id=(w, v),
            device_id_type=MESH,
        ).start()

    def send_class(half, base, steps, offsets):
        def body(i, carry):
            listed = offsets(i)
            for n, offset in enumerate(listed):
                send_to(half, base + len(listed) * i + n, offset)
            return carry

        lax.fori_loop(0, steps, body, 0)

    pl.semaphore_wait(barrier, len(near_by))
    hello(hello_sem.at[0])
    for n, offset in enumerate(near_by):
        send_to(0, 1 + n, offset)
    pl.semaphore_wait(hello_sem.at[0], len(near_by))
    hello(hello_sem.at[1])
    send_class(0, *classes[0])
    pl.semaphore_wait(hello_sem.at[1], len(near_by))
    hello(hello_sem.at[2])
    send_class(0, *classes[1])
    pl.semaphore_wait(hello_sem.at[2], len(near_by))
    send_class(0, *classes[2])
    pack(0, got_a.at[0], me)
    pack(1, got_b.at[0], me)
    for n, offset in enumerate(near_by):
        send_to(1, 1 + n, offset)
    for arguments in classes:
        send_class(1, *arguments)

    tile_row = lax.broadcasted_iota(jnp.int32, (16, CN), 0).astype(f32)
    row16 = tile_row.astype(bf16)
    none, one = jnp.zeros((16, CN), bf16), jnp.ones((16, CN), bf16)

    def place_of(cells):
        i = jnp.floor((cells + 0.5) * (1.0 / COLS))
        j = cells - i * COLS - 1.0
        return i, jnp.where(j < 0.0, COLS - 1.0, j)

    def fill_hot(hot_buf, j, lane_at):
        j16 = jnp.broadcast_to(j, (16, CN)).astype(bf16)
        for t in range(-(-COLS // 16)):
            hot_buf[16 * t : 16 * t + 16, lane_at : lane_at + CN] = jnp.where(
                row16 + jnp.full((16, CN), 16 * t, bf16) == j16, one, none
            )

    def two_terms(value):
        high = value.astype(bf16).astype(f32)
        return jnp.concatenate([high, value - high], axis=0).astype(bf16)

    def build(half, p0, left_buf, hot_buf):
        for n in range(GROUP):
            for slot in range(2):
                at = (2 * n + slot) * CN
                p = p0 + n
                i, j = place_of(got_a[p, 18 + slot : 19 + slot, :])
                fill_hot(hot_buf, j, at)
                terms = two_terms(gots[half][p, 8 * slot : 8 * slot + 8, :])
                i16 = jnp.broadcast_to(i, (16, CN)).astype(bf16)
                for r in range(ROWS):
                    left_buf[16 * r : 16 * r + 16, at : at + CN] = jnp.where(
                        i16 == jnp.full((16, CN), r, bf16), terms, none
                    )
                if half == 0:
                    m16 = jnp.broadcast_to(got_a[p, 16 + slot : 17 + slot, :], (16, CN))
                    mhi = m16.astype(bf16)
                    mlo = (m16 - mhi.astype(f32)).astype(bf16)
                    mask = i16 == row16
                    left_buf[160:176, at : at + CN] = jnp.where(mask, mhi, none)
                    left_buf[176:192, at : at + CN] = jnp.where(mask, mlo, none)

    def add_up(half, left_buf, hot_buf):
        rows = accs[half].shape[0]
        accs[half][...] += lax.dot_general(
            left_buf[0:rows, :],
            hot_buf[...],
            (((1,), (1,)), ((), ())),
            preferred_element_type=f32,
        )

    def deposit(half, t, first=0):
        p = t * PAIR
        span = pl.ds(p + first, PAIR - first)
        pltpu.make_async_copy(
            outs[half].at[span], gots[half].at[span], recv_sem.at[half, t]
        ).wait()
        build(half, p, left_even, hot_even)
        build(half, p + GROUP, left_odd, hot_odd)
        add_up(half, left_even, hot_even)
        add_up(half, left_odd, hot_odd)

    def deposit_range(half, low, high):
        def body(t, carry):
            deposit(half, t)
            return carry

        lax.fori_loop(low, high, body, 0)

    above, below = (wide + 15) % 16, (wide + 1) % 16
    before, after = (narrow + 7) % 8, (narrow + 1) % 8
    at_lanes = [
        lax.broadcasted_iota(jnp.int32, (tile.shape[0], 128), 1) for tile in tiles
    ]

    def halo_copies(half):
        tile_ref, side_buf = tiles[half], (side_a, side_b)[half]
        up, side_got, diag = ((up_a, side_got_a, diag_a), (up_b, side_got_b, diag_b))[half]
        rows, edge = tile_ref.shape[0], up.shape[1]
        top, bottom = pl.ds(0, edge), pl.ds(rows - edge, edge)
        listed = [
            (tile_ref.at[top], up.at[1], (above, narrow)),
            (tile_ref.at[bottom], up.at[0], (below, narrow)),
            (side_buf.at[0], side_got.at[1], (wide, before)),
            (side_buf.at[1], side_got.at[0], (wide, after)),
            (side_buf.at[0, top], diag.at[3], (above, before)),
            (side_buf.at[0, bottom], diag.at[1], (below, before)),
            (side_buf.at[1, top], diag.at[2], (above, after)),
            (side_buf.at[1, bottom], diag.at[0], (below, after)),
        ]
        return [
            pltpu.make_async_remote_copy(
                src,
                dst,
                halo_send.at[half, n],
                halo_recv.at[half, n],
                device_id=to,
                device_id_type=MESH,
            )
            for n, (src, dst, to) in enumerate(listed)
        ]

    def halo_start(half):
        acc, tile_ref, side_buf = accs[half], tiles[half], (side_a, side_b)[half]
        start = 8 if half == 0 else 0
        for r in range(ROWS):
            tile_ref[start + 8 * r : start + 8 * r + 8, :] = (
                acc[16 * r : 16 * r + 8, :] + acc[16 * r + 8 : 16 * r + 16, :]
            )
        if half == 0:
            tile_ref[0:8, :] = acc[160:168, :] + acc[176:184, :]
            tile_ref[88:96, :] = acc[168:176, :] + acc[184:192, :]
        own, rest = tile_ref[:, 0:128], tile_ref[:, 128:256]
        at_lane = at_lanes[half]
        side_buf[0] = jnp.where(at_lane == 127, pltpu.roll(rest, 126, 1), own)
        side_buf[1] = jnp.where(at_lane == 0, rest, pltpu.roll(own, 2, 1))
        for copy in halo_copies(half):
            copy.start()

    def halo_finish(half):
        for copy in halo_copies(half):
            copy.wait()
        tile_ref, at_lane = tiles[half], at_lanes[half]
        up, side_got, diag = ((up_a, side_got_a, diag_a), (up_b, side_got_b, diag_b))[half]

        def unfold(high, low):
            middle = jnp.zeros((48, high.shape[1]), f32)
            if half == 0:
                parts = [high[16:24], high[0:16], middle, low[8:24], low[0:8]]
            else:
                parts = [high, middle, low]
            return jnp.concatenate(parts, axis=0)

        from_left = side_got[0] + unfold(diag[0], diag[2])
        from_right = side_got[1] + unfold(diag[1], diag[3])
        vertical = unfold(up[0], up[1])
        own = (
            tile_ref[:, 0:128]
            + vertical[:, 0:128]
            + jnp.where(at_lane == 0, from_left, 0.0)
            + jnp.where(at_lane == 127, from_right, 0.0)
        )
        rest = (
            tile_ref[:, 128:256]
            + vertical[:, 128:256]
            + jnp.where(at_lane == 1, from_left, 0.0)
            + jnp.where(at_lane == 0, from_right, 0.0)
        )
        total = jnp.concatenate([own, rest], axis=1)
        if half == 0:
            inverse_ref[0:8, :] = 1.0 / (total[0:8, :] + 1.0)
            inverse_ref[8:16, :] = 1.0 / (total[88:96, :] + 1.0)
        start = 8 if half == 0 else 0
        for r in range(ROWS):
            mean = total[start + 8 * r : start + 8 * r + 8, :] * inverse_ref[r : r + 1, :]
            if 1 <= r <= CW:
                mean_ref[8 * half : 8 * half + 8, r - 1, :] = mean[:, 0:CN]
            means[half][16 * r : 16 * r + 16, :] = two_terms(mean)

    def lookup(half, p, count, hot_buf):
        rows = []
        for n in range(count):
            for slot in range(2):
                i, j = place_of(got_a[p + n, 18 + slot : 19 + slot, :])
                fill_hot(hot_buf, j, (2 * n + slot) * CN)
                rows.append(i)
        for n in range(count):
            found = jnp.dot(
                means[half][...],
                hot_buf[:, 256 * n : 256 * n + 256],
                preferred_element_type=f32,
            )
            for slot in range(2):
                i8 = jnp.broadcast_to(rows[2 * n + slot], (8, CN))
                near = jnp.zeros((8, CN), f32)
                cut = slice(CN * slot, CN * slot + CN)
                for r in range(ROWS):
                    near = near + jnp.where(
                        i8 == float(r),
                        found[16 * r : 16 * r + 8, cut] + found[16 * r + 8 : 16 * r + 16, cut],
                        0.0,
                    )
                nears[half][2 * (p + n) + slot] = near

    def give_back(half, p, offset):
        pltpu.make_async_remote_copy(
            nears[half].at[pl.ds(2 * p, 2)],
            rets[half].at[pl.ds(2 * me, 2)],
            back_send.at[half],
            back_recv.at[half],
            device_id=at_offset(offset, -1),
            device_id_type=MESH,
        ).start()

    hot_bufs = (hot_even, hot_odd)

    def return_class(half, base, steps, offsets):
        def body(i, carry):
            listed = offsets(i)
            p = base + len(listed) * i
            for n in range(0, len(listed), 3):
                some = listed[n : n + 3]
                lookup(half, p + n, len(some), hot_bufs[(n // 3) % 2])
                for m, offset in enumerate(some):
                    give_back(half, p + n + m, offset)
            return carry

        lax.fori_loop(0, steps, body, 0)

    def return_near(half):
        for p in (8, 4, 0):
            lookup(half, p, min(4, 11 - p), hot_bufs[(p // 4) % 2])
            for n in range(p, min(p + 4, 11)):
                if n:
                    give_back(half, n, near_by[n - 1])
        rets[half][pl.ds(2 * me, 2)] = nears[half][0:2]

    pairs = devices // PAIR
    deposit(0, 0, 1)
    deposit_range(0, 1, pairs)
    halo_start(0)
    deposit(1, 0, 1)
    deposit_range(1, 1, EARLY)
    halo_finish(0)
    return_class(0, *classes[2])
    return_class(0, *classes[1])
    deposit_range(1, EARLY, pairs)
    halo_start(1)
    return_class(0, *classes[0])
    return_near(0)
    halo_finish(1)
    for arguments in reversed(classes):
        return_class(1, *arguments)
    return_near(1)

    others = pl.ds(2, 2 * (devices - 1))

    def returned(half):
        pltpu.make_async_copy(
            nears[half].at[others], rets[half].at[others], back_recv.at[half]
        ).wait()

    returned(0)

    def read_rate(b, carry):
        row_buf[pl.ds(b, 1), :] = ret_a[idx_sm[4, b], 0:1, :]
        return carry

    lax.fori_loop(0, lanes, read_rate, 0, unroll=8)
    row_buf[...] = jnp.exp(-freq_ref[...] * (1.5 + jnp.tanh(row_buf[...])))

    def mix(half):
        def body(b, carry):
            near = rets[half][idx_sm[4, b]]
            own = scal_ref[b, 8 * half : 8 * half + 8, :]
            mixed_ref[b, 8 * half : 8 * half + 8, :] = near + (own - near) * row_buf[pl.ds(b, 1), :]
            return carry

        lax.fori_loop(0, lanes, body, 0, unroll=8)

    mix(0)
    returned(1)
    mix(1)

    for half in range(2):
        rest_of = pl.ds(1, devices - 1)
        pltpu.make_async_copy(
            outs[half].at[rest_of], gots[half].at[rest_of], send_sem.at[half]
        ).wait()
        pltpu.make_async_copy(
            nears[half].at[others], rets[half].at[others], back_send.at[half]
        ).wait()


def per_device(scalars, mass, frequency, cell, owner):
    devices = lax.axis_size("wide") * lax.axis_size("narrow")
    blocks, count, per_block = scalars.shape
    f32, bf16 = jnp.float32, jnp.bfloat16
    vmem = pl.BlockSpec(memory_space=pltpu.VMEM)
    return pl.pallas_call(
        functools.partial(kernel, devices),
        out_shape=(
            jax.ShapeDtypeStruct((blocks, count, per_block), f32),
            jax.ShapeDtypeStruct((count, CW, CN), f32),
        ),
        in_specs=[pl.BlockSpec(memory_space=pltpu.HBM)] * 5,
        out_specs=(vmem, vmem),
        scratch_shapes=[
            pltpu.VMEM((devices, 20, per_block), f32),
            pltpu.VMEM((devices, 16, per_block), f32),
            pltpu.VMEM((devices, 20, per_block), f32),
            pltpu.VMEM((devices, 16, per_block), f32),
            *[pltpu.VMEM((2 * devices, 8, per_block), f32)] * 4,
            pltpu.VMEM((blocks, count, per_block), f32),
            pltpu.VMEM((blocks, per_block), f32),
            pltpu.VMEM((blocks, per_block), jnp.int32),
            pltpu.VMEM((1, blocks), jnp.int32),
            pltpu.VMEM((192, GROUP * 256), bf16),
            pltpu.VMEM((192, GROUP * 256), bf16),
            pltpu.VMEM((256, GROUP * 256), bf16),
            pltpu.VMEM((256, GROUP * 256), bf16),
            pltpu.VMEM((192, 256), f32),
            pltpu.VMEM((160, 256), f32),
            pltpu.VMEM((96, 256), f32),
            pltpu.VMEM((80, 256), f32),
            pltpu.VMEM((2, 96, 128), f32),
            pltpu.VMEM((2, 80, 128), f32),
            pltpu.VMEM((2, 24, 256), f32),
            pltpu.VMEM((2, 16, 256), f32),
            pltpu.VMEM((2, 96, 128), f32),
            pltpu.VMEM((2, 80, 128), f32),
            pltpu.VMEM((4, 24, 128), f32),
            pltpu.VMEM((4, 16, 128), f32),
            pltpu.VMEM((160, 256), bf16),
            pltpu.VMEM((160, 256), bf16),
            pltpu.VMEM((16, 256), f32),
            pltpu.VMEM((8, blocks), jnp.int32),
            pltpu.SMEM((8, blocks), jnp.int32),
            pltpu.VMEM((blocks, per_block), f32),
            pltpu.VMEM((blocks + 8, per_block), f32),
            pltpu.SemaphoreType.DMA((5,)),
            pltpu.SemaphoreType.REGULAR((3,)),
            pltpu.SemaphoreType.DMA,
            pltpu.SemaphoreType.DMA((2,)),
            pltpu.SemaphoreType.DMA((2, devices // PAIR)),
            pltpu.SemaphoreType.DMA((2,)),
            pltpu.SemaphoreType.DMA((2,)),
            pltpu.SemaphoreType.DMA((2, 8)),
            pltpu.SemaphoreType.DMA((2, 8)),
        ],
        compiler_params=pltpu.CompilerParams(
            collective_id=0, has_side_effects=True, vmem_limit_bytes=64 << 20
        ),
        name="mixing",
    )(scalars, mass, frequency, cell, owner.reshape(1, blocks))


def solution(mesh):
    held = P(("wide", "narrow"), None)
    block = P(("wide", "narrow"), None, None)
    return jax.shard_map(
        per_device,
        mesh=mesh,
        in_specs=(block, held, held, held, held),
        out_specs=(block, P(None, "wide", "narrow")),
        check_vma=False,
    )
```

time: 82.2 us -> 77.7 us (0.945)
  Pallas kernels: 78.5 us -> 74 us
    pallas_call x1, Pallas kernels: 78.5 us -> 74 us  [per_device(): pl.pallas_call(functools.partial(kernel, devices), out_shape=(jax.ShapeDt...]
where the time goes in v3:
time: 77.7 us; the launch traced here: 77.5 us
  Pallas kernels  74 us (95%)
  local copies, waits for them, and re-layouts  2.93 us (4%)
    pallas_call x1, Pallas kernels, per_device(): pl.pallas_call(functools.partial(kernel, devices), out_shape=(jax.ShapeDt...  74 us
    unnamed x4, local copies, waits for them, and re-layouts  2.93 us

profile of v3, /device:TPU:1, one launch (start us, length us, event | category | flops | bytes accessed | tf_op | source)
XLA Modules:
  0.0 77.5 jit_solution(15873504490347475047)
XLA Ops:
  0.6 74.0 %mixing.1 = (f32[128,16,128]{2,1,0:T(8,128)}, f32[16,8,128]{2,1,0:T(8,128)}) custom-call(f32[128,16,128]{2,1,0:T(8,128)} %scal_hbm.1, f32[128,128]{1,0:T(8,128)} %mass_hbm.1, f32[128,128]{1,0:T(8,128)} %freq_hbm.1, s32[128,128]{1,0:T(8,128)} %cell_hbm.1, s32[1,128]{1,0:T(1,128)} %bitcast.1), custom_call_target="tpu_custom_call" | custom-call | tf_op jit(solution)/shard_map/mixing/pallas_call | solution.py:486
  74.6 0.0 copy-start
  74.6 2.3 %copy.9 = f32[128,16,128]{2,1,0:T(8,128)} copy(f32[128,16,128]{2,1,0:T(8,128)} %get-tuple-element.4) | data formatting | bytes 2097152
  76.9 0.0 copy-done
  76.9 0.6 copy.10
Async XLA Ops:
  74.6 2.3 %copy-start = (f32[16,8,128]{2,1,0:T(8,128)S(1)}, f32[16,8,128]{2,1,0:T(8,128)}, u32[]{:S(2)}) copy-start(f32[16,8,128]{2,1,0:T(8,128)} %get-tuple-element.5) | copy-start | bytes 196612

commit v4 on v3

--- a/solution.py
+++ b/solution.py
@@ -14,7 +14,7 @@
 MESH = pl.DeviceIdType.MESH
 GROUP = 4
 PAIR = 2 * GROUP
-EARLY = 14
+EARLY = 11
 
 
 def kernel(
@@ -40,8 +40,7 @@
     owner_ref,
     left_even,
     left_odd,
-    hot_even,
-    hot_odd,
+    hot_ref,
     acc_a,
     acc_b,
     tile_a,
@@ -98,10 +97,10 @@
         return [last[0], (a, b, 0, 1), last[1], (b, 0, a, 1), last[2], (0, a, b, 1)]
 
     def four_axes(i):
-        a, b = 1 + lax.div(i, 3), 1 + lax.rem(i, 3)
-        return [(a, b, n, 1) for n in (1, 2, 3)]
-
-    classes = [(11, 9, two_axes), (47, 9, three_axes), (101, 9, four_axes)]
+        a = 1 + i
+        return [(a, b, 1 + (b + n) % 3, 1) for n in range(3) for b in (1, 2, 3)]
+
+    classes = [(11, 9, two_axes), (47, 9, three_axes), (101, 3, four_axes)]
 
     def hello(sem):
         for offset in near_by:
@@ -128,8 +127,6 @@
     weight_ref[lanes : lanes + 8, :] = jnp.zeros((8, CN), f32)
     acc_a[...] = jnp.zeros_like(acc_a)
     acc_b[...] = jnp.zeros_like(acc_b)
-    for hot_buf in (hot_even, hot_odd):
-        hot_buf[144:256, :] = jnp.zeros((112, hot_buf.shape[1]), bf16)
     loads[0].wait()
     along = jnp.broadcast_to(owner_ref[...], (lanes, lanes))
     down = along.T
@@ -214,10 +211,10 @@
         j = cells - i * COLS - 1.0
         return i, jnp.where(j < 0.0, COLS - 1.0, j)
 
-    def fill_hot(hot_buf, j, lane_at):
+    def fill_hot(p, slot, j):
         j16 = jnp.broadcast_to(j, (16, CN)).astype(bf16)
         for t in range(-(-COLS // 16)):
-            hot_buf[16 * t : 16 * t + 16, lane_at : lane_at + CN] = jnp.where(
+            hot_ref[p, 16 * t : 16 * t + 16, CN * slot : CN * slot + CN] = jnp.where(
                 row16 + jnp.full((16, CN), 16 * t, bf16) == j16, one, none
             )
 
@@ -225,13 +222,14 @@
         high = value.astype(bf16).astype(f32)
         return jnp.concatenate([high, value - high], axis=0).astype(bf16)
 
-    def build(half, p0, left_buf, hot_buf):
+    def build(half, p0, left_buf):
         for n in range(GROUP):
             for slot in range(2):
                 at = (2 * n + slot) * CN
                 p = p0 + n
                 i, j = place_of(got_a[p, 18 + slot : 19 + slot, :])
-                fill_hot(hot_buf, j, at)
+                if half == 0:
+                    fill_hot(p, slot, j)
                 terms = two_terms(gots[half][p, 8 * slot : 8 * slot + 8, :])
                 i16 = jnp.broadcast_to(i, (16, CN)).astype(bf16)
                 for r in range(ROWS):
@@ -246,14 +244,15 @@
                     left_buf[160:176, at : at + CN] = jnp.where(mask, mhi, none)
                     left_buf[176:192, at : at + CN] = jnp.where(mask, mlo, none)
 
-    def add_up(half, left_buf, hot_buf):
+    def add_up(half, p0, left_buf):
         rows = accs[half].shape[0]
-        accs[half][...] += lax.dot_general(
-            left_buf[0:rows, :],
-            hot_buf[...],
-            (((1,), (1,)), ((), ())),
-            preferred_element_type=f32,
-        )
+        for n in range(GROUP):
+            accs[half][:, 0:144] += lax.dot_general(
+                left_buf[0:rows, 256 * n : 256 * n + 256],
+                hot_ref[p0 + n],
+                (((1,), (1,)), ((), ())),
+                preferred_element_type=f32,
+            )
 
     def deposit(half, t, first=0):
         p = t * PAIR
@@ -261,10 +260,10 @@
         pltpu.make_async_copy(
             outs[half].at[span], gots[half].at[span], recv_sem.at[half, t]
         ).wait()
-        build(half, p, left_even, hot_even)
-        build(half, p + GROUP, left_odd, hot_odd)
-        add_up(half, left_even, hot_even)
-        add_up(half, left_odd, hot_odd)
+        build(half, p, left_even)
+        build(half, p + GROUP, left_odd)
+        add_up(half, p, left_even)
+        add_up(half, p + GROUP, left_odd)
 
     def deposit_range(half, low, high):
         def body(t, carry):
@@ -363,30 +362,19 @@
                 mean_ref[8 * half : 8 * half + 8, r - 1, :] = mean[:, 0:CN]
             means[half][16 * r : 16 * r + 16, :] = two_terms(mean)
 
-    def lookup(half, p, count, hot_buf):
-        rows = []
-        for n in range(count):
-            for slot in range(2):
-                i, j = place_of(got_a[p + n, 18 + slot : 19 + slot, :])
-                fill_hot(hot_buf, j, (2 * n + slot) * CN)
-                rows.append(i)
+    def lookup(half, p, count):
         for n in range(count):
             found = jnp.dot(
-                means[half][...],
-                hot_buf[:, 256 * n : 256 * n + 256],
-                preferred_element_type=f32,
+                means[half][:, 0:144], hot_ref[p + n], preferred_element_type=f32
             )
             for slot in range(2):
-                i8 = jnp.broadcast_to(rows[2 * n + slot], (8, CN))
-                near = jnp.zeros((8, CN), f32)
+                i, _ = place_of(got_a[p + n, 18 + slot : 19 + slot, :])
+                i16 = jnp.broadcast_to(i, (16, CN))
                 cut = slice(CN * slot, CN * slot + CN)
-                for r in range(ROWS):
-                    near = near + jnp.where(
-                        i8 == float(r),
-                        found[16 * r : 16 * r + 8, cut] + found[16 * r + 8 : 16 * r + 16, cut],
-                        0.0,
-                    )
-                nears[half][2 * (p + n) + slot] = near
+                near = found[0:16, cut]
+                for r in range(1, ROWS):
+                    near = jnp.where(i16 == float(r), found[16 * r : 16 * r + 16, cut], near)
+                nears[half][2 * (p + n) + slot] = near[0:8] + near[8:16]
 
     def give_back(half, p, offset):
         pltpu.make_async_remote_copy(
@@ -398,24 +386,20 @@
             device_id_type=MESH,
         ).start()
 
-    hot_bufs = (hot_even, hot_odd)
-
     def return_class(half, base, steps, offsets):
         def body(i, carry):
             listed = offsets(i)
             p = base + len(listed) * i
-            for n in range(0, len(listed), 3):
-                some = listed[n : n + 3]
-                lookup(half, p + n, len(some), hot_bufs[(n // 3) % 2])
-                for m, offset in enumerate(some):
-                    give_back(half, p + n + m, offset)
+            lookup(half, p, len(listed))
+            for n, offset in enumerate(listed):
+                give_back(half, p + n, offset)
             return carry
 
         lax.fori_loop(0, steps, body, 0)
 
     def return_near(half):
         for p in (8, 4, 0):
-            lookup(half, p, min(4, 11 - p), hot_bufs[(p // 4) % 2])
+            lookup(half, p, min(4, 11 - p))
             for n in range(p, min(p + 4, 11)):
                 if n:
                     give_back(half, n, near_by[n - 1])
@@ -503,8 +487,7 @@
             pltpu.VMEM((1, blocks), jnp.int32),
             pltpu.VMEM((192, GROUP * 256), bf16),
             pltpu.VMEM((192, GROUP * 256), bf16),
-            pltpu.VMEM((256, GROUP * 256), bf16),
-            pltpu.VMEM((256, GROUP * 256), bf16),
+            pltpu.VMEM((devices, 144, 256), bf16),
             pltpu.VMEM((192, 256), f32),
             pltpu.VMEM((160, 256), f32),
             pltpu.VMEM((96, 256), f32),

time: 77.7 us -> 74.2 us (0.955)
  Pallas kernels: 74 us -> 70.5 us
    pallas_call x1, Pallas kernels: 74 us -> 70.5 us  [per_device(): pl.pallas_call(functools.partial(kernel, devices), out_shape=(jax.ShapeDt...]
where the time goes in v4:
time: 74.2 us; the launch traced here: 74.1 us
  Pallas kernels  70.5 us (95%)
  local copies, waits for them, and re-layouts  2.93 us (4%)
    pallas_call x1, Pallas kernels, per_device(): pl.pallas_call(functools.partial(kernel, devices), out_shape=(jax.ShapeDt...  70.5 us
    unnamed x4, local copies, waits for them, and re-layouts  2.93 us

profile of v4, /device:TPU:1, one launch (start us, length us, event | category | flops | bytes accessed | tf_op | source)
XLA Modules:
  0.0 74.1 jit_solution(1629042017332497485)
XLA Ops:
  0.6 70.5 %mixing.1 = (f32[128,16,128]{2,1,0:T(8,128)}, f32[16,8,128]{2,1,0:T(8,128)}) custom-call(f32[128,16,128]{2,1,0:T(8,128)} %scal_hbm.1, f32[128,128]{1,0:T(8,128)} %mass_hbm.1, f32[128,128]{1,0:T(8,128)} %freq_hbm.1, s32[128,128]{1,0:T(8,128)} %cell_hbm.1, s32[1,128]{1,0:T(1,128)} %bitcast.1), custom_call_target="tpu_custom_call" | custom-call | tf_op jit(solution)/shard_map/mixing/pallas_call | solution.py:470
  71.1 0.0 copy-start
  71.1 2.3 %copy.9 = f32[128,16,128]{2,1,0:T(8,128)} copy(f32[128,16,128]{2,1,0:T(8,128)} %get-tuple-element.4) | data formatting | bytes 2097152
  73.4 0.0 copy-done
  73.4 0.6 copy.10
Async XLA Ops:
  71.1 2.3 %copy-start = (f32[16,8,128]{2,1,0:T(8,128)S(1)}, f32[16,8,128]{2,1,0:T(8,128)}, u32[]{:S(2)}) copy-start(f32[16,8,128]{2,1,0:T(8,128)} %get-tuple-element.5) | copy-start | bytes 196612

commit v5 on v4

--- a/solution.py
+++ b/solution.py
@@ -24,8 +24,8 @@
     freq_hbm,
     cell_hbm,
     owner_hbm,
-    mixed_ref,
-    mean_ref,
+    mixed_hbm,
+    mean_hbm,
     out_a,
     out_b,
     got_a,
@@ -60,6 +60,9 @@
     idx_sm,
     row_buf,
     weight_ref,
+    mixed_ref,
+    mean_ref,
+    store_sem,
     load_sem,
     hello_sem,
     idx_sem,
@@ -419,6 +422,8 @@
     return_class(0, *classes[0])
     return_near(0)
     halo_finish(1)
+    stores = [pltpu.make_async_copy(mean_ref, mean_hbm, store_sem.at[2])]
+    stores[0].start()
     for arguments in reversed(classes):
         return_class(1, *arguments)
     return_near(1)
@@ -448,9 +453,19 @@
 
         lax.fori_loop(0, lanes, body, 0, unroll=8)
 
+    def store(half):
+        rows = pl.ds(8 * half, 8)
+        copy = pltpu.make_async_copy(
+            mixed_ref.at[:, rows], mixed_hbm.at[:, rows], store_sem.at[half]
+        )
+        copy.start()
+        stores.append(copy)
+
     mix(0)
+    store(0)
     returned(1)
     mix(1)
+    store(1)
 
     for half in range(2):
         rest_of = pl.ds(1, devices - 1)
@@ -460,21 +475,23 @@
         pltpu.make_async_copy(
             nears[half].at[others], rets[half].at[others], back_send.at[half]
         ).wait()
+    for copy in stores:
+        copy.wait()
 
 
 def per_device(scalars, mass, frequency, cell, owner):
     devices = lax.axis_size("wide") * lax.axis_size("narrow")
     blocks, count, per_block = scalars.shape
     f32, bf16 = jnp.float32, jnp.bfloat16
-    vmem = pl.BlockSpec(memory_space=pltpu.VMEM)
+    hbm = pl.BlockSpec(memory_space=pltpu.HBM)
     return pl.pallas_call(
         functools.partial(kernel, devices),
         out_shape=(
             jax.ShapeDtypeStruct((blocks, count, per_block), f32),
             jax.ShapeDtypeStruct((count, CW, CN), f32),
         ),
-        in_specs=[pl.BlockSpec(memory_space=pltpu.HBM)] * 5,
-        out_specs=(vmem, vmem),
+        in_specs=[hbm] * 5,
+        out_specs=(hbm, hbm),
         scratch_shapes=[
             pltpu.VMEM((devices, 20, per_block), f32),
             pltpu.VMEM((devices, 16, per_block), f32),
@@ -507,6 +524,9 @@
             pltpu.SMEM((8, blocks), jnp.int32),
             pltpu.VMEM((blocks, per_block), f32),
             pltpu.VMEM((blocks + 8, per_block), f32),
+            pltpu.VMEM((blocks, count, per_block), f32),
+            pltpu.VMEM((count, CW, CN), f32),
+            pltpu.SemaphoreType.DMA((3,)),
             pltpu.SemaphoreType.DMA((5,)),
             pltpu.SemaphoreType.REGULAR((3,)),
             pltpu.SemaphoreType.DMA,

time: 74.2 us -> 74.1 us (level)
  no operation moved by 1% of the time
where the time goes in v5:
time: 74.1 us; the launch traced here: 73.9 us
  Pallas kernels  70.3 us (95%)
  local copies, waits for them, and re-layouts  2.93 us (4%)
    pallas_call x1, Pallas kernels, per_device(): pl.pallas_call(functools.partial(kernel, devices), out_shape=(jax.ShapeDt...  70.3 us
    unnamed x4, local copies, waits for them, and re-layouts  2.93 us

profile of v5, /device:TPU:1, one launch (start us, length us, event | category | flops | bytes accessed | tf_op | source)
XLA Modules:
  0.0 73.9 jit_solution(5384021405537732248)
XLA Ops:
  0.6 70.3 %mixing.1 = (f32[128,16,128]{2,1,0:T(8,128)}, f32[16,8,128]{2,1,0:T(8,128)}) custom-call(f32[128,16,128]{2,1,0:T(8,128)} %scal_hbm.1, f32[128,128]{1,0:T(8,128)} %mass_hbm.1, f32[128,128]{1,0:T(8,128)} %freq_hbm.1, s32[128,128]{1,0:T(8,128)} %cell_hbm.1, s32[1,128]{1,0:T(1,128)} %bitcast.1), custom_call_target="tpu_custom_call" | custom-call | tf_op jit(solution)/shard_map/mixing/pallas_call | solution.py:487
  71.0 0.0 copy-start
  71.0 2.3 %copy.9 = f32[128,16,128]{2,1,0:T(8,128)} copy(f32[128,16,128]{2,1,0:T(8,128)} %get-tuple-element.4) | data formatting | bytes 2097152
  73.3 0.0 copy-done
  73.3 0.6 copy.10
Async XLA Ops:
  71.0 2.3 %copy-start = (f32[16,8,128]{2,1,0:T(8,128)S(1)}, f32[16,8,128]{2,1,0:T(8,128)}, u32[]{:S(2)}) copy-start(f32[16,8,128]{2,1,0:T(8,128)} %get-tuple-element.5) | copy-start | bytes 196612
